TPU v7x, 512 devices: a whole 4x4x16 slice. The times are simulated.
512 devices in a mesh: irrep: 8 (over y, core), tile: 64 (over z, x).
Axes of the slice: x: 4, y: 4, z: 16, core: 2. Of those that a mesh axis runs over, the one named last changes fastest.
Arguments:
- amplitudes: bfloat16 [8, 1024, 64, 256], P('irrep', 'tile'), may hold values from -6 to 6
- integrals: bfloat16 [8, 64, 256, 256], P('irrep', 'tile'), may hold values from -0.375 to 0.375
- executors: int32 [8, 1024, 2], P('irrep', 'tile'), may hold values from 0 to 63, all different within a row; in each aligned block of 16 rows (0 to 15, 16 to 31, ..., all dimensions but the last counted through in order) at most 2 rows name the same one
- residual_slots: int32 [8, 1024, 2], P('irrep', 'tile'), may hold values from 0 to 7
Outputs:
- residual: bfloat16 [8, 512, 64, 256], P('irrep', 'tile')
Inputs may be any that keep to these rules, and one draw needn't show every extreme that they name: `executors`: within a row the 2 entries differ. Within the 16 rows of one device no value appears more than 2 times.
All inputs are finite; a program needn't handle non-finite values.
Results may differ from a plain program's by a relative error of at most 0.005.
Values may be sent and summed in bfloat16 or wider, within the bound.
No kernel may reach another device: no remote copies, remote signals or barrier semaphores. Data moves between devices by JAX's collectives and lax.ppermute only.
A program may use at most 64 MiB of HBM per device.

v0:
```python
import jax
import jax.numpy as jnp
from jax import lax
from jax.sharding import PartitionSpec as P

RT = 8


def swapped(block, axis, stride):
    count = lax.axis_size(axis)
    route = []
    for low in range(count):
        high = low | 1 << stride
        if high != low and high < count:
            route += [(low, high), (high, low)]
    return lax.ppermute(block, axis, route)


def per_device(amplitudes, integrals, executors, residual_slots):
    tile_count = lax.axis_size("tile")
    own_count = amplitudes.shape[1]
    row_count = amplitudes.shape[2]
    columns = amplitudes.shape[3]
    fanout = executors.shape[2]
    task_count = own_count * fanout
    capacity = max(2, 2 * own_count * fanout // tile_count)
    theirs = swapped(integrals, "irrep", 0)
    targets = executors.reshape(task_count)
    slots = residual_slots.reshape(task_count)
    slot_hot = (slots[:, None] == jnp.arange(RT, dtype=jnp.int32)).astype(jnp.bfloat16)
    target_hot = (targets[:, None] == jnp.arange(tile_count, dtype=jnp.int32)).astype(jnp.int32)
    earlier = jnp.cumsum(target_hot, axis=0) - target_hot
    position = jnp.sum(earlier * target_hot, axis=1)
    slot_count = tile_count * capacity
    placed = targets * capacity + position
    place_hot = (placed[:, None] == jnp.arange(slot_count, dtype=jnp.int32)).astype(jnp.bfloat16)
    owner_index = jnp.arange(task_count, dtype=jnp.int32) // fanout
    owner_hot = (owner_index[:, None] == jnp.arange(own_count, dtype=jnp.int32)).astype(
        jnp.bfloat16
    )
    picker = jnp.dot(place_hot.T, owner_hot, preferred_element_type=jnp.float32).astype(
        jnp.bfloat16
    )
    flat_own = amplitudes.reshape(own_count, row_count * columns)
    outbox = jnp.dot(picker, flat_own, preferred_element_type=jnp.float32).astype(jnp.bfloat16)
    outbox = outbox.reshape(tile_count, capacity, row_count, columns)
    partner_tile = theirs[0, 0]
    partial_value = jnp.einsum(
        "scrw,wv->scrv",
        lax.all_to_all(outbox, "tile", split_axis=0, concat_axis=0, tiled=True),
        partner_tile,
        preferred_element_type=jnp.float32,
    ).astype(jnp.bfloat16)
    returned = lax.all_to_all(partial_value, "tile", split_axis=0, concat_axis=0, tiled=True)
    collect = jnp.dot(slot_hot.T, place_hot, preferred_element_type=jnp.float32).astype(
        jnp.bfloat16
    )
    summed = jnp.dot(
        collect,
        returned.reshape(slot_count, row_count * columns),
        preferred_element_type=jnp.float32,
    )
    return summed.astype(jnp.bfloat16).reshape(1, RT, row_count, columns)


def solution(mesh):
    placed = (
        P("irrep", "tile", None, None),
        P("irrep", "tile", None, None),
        P("irrep", "tile", None),
        P("irrep", "tile", None),
    )
    return jax.shard_map(
        per_device,
        mesh=mesh,
        in_specs=placed,
        out_specs=P("irrep", "tile", None, None),
        check_vma=False,
    )
```

profile of v0, /device:TPU:24, one launch (start us, length us, event | category | flops | bytes accessed | tf_op | source)
XLA Modules:
  0.0 432.2 jit_solution(17176949130987170007)
XLA Ops:
  0.0 0.8 copy.9
  0.8 0.1 reshape.38
  0.8 0.1 fusion.1
  0.9 0.1 reduce_window_sum.11
  1.0 0.2 select_reduce_fusion
  1.2 1.3 copy.12
  2.5 3.4 convolution_convert_fusion
  5.9 5.4 %copy.13 = bf16[16,8,64,256]{3,2,1,0:T(8,128)(2,1)} copy(bf16[16,8,64,256]{3,1,2,0:T(8,128)(2,1)} %bitcast.20) | data formatting | bytes 8388608
  11.3 0.0 copy-start.1
  11.3 19.0 %all-to-all-start = ((bf16[64,2,64,256]{3,2,1,0:T(8,128)(2,1)}), bf16[64,2,64,256]{3,2,1,0:T(8,128)(2,1)}, u32[]{:S(2)}, u32[]{:S(2)}) async-start(bf16[64,2,64,256]{3,2,1,0:T(8,128)(2,1)} %bitcast.21), calls=%async_computation | async-start | bytes 8388608 | tf_op jit(solution)/shard_map/all_to_all | solution.py:50
  30.3 0.0 copy-done.1
  30.3 1.9 collective-permute-start
  32.2 1.3 collective-permute-done
  33.5 186.7 %all-to-all-done = bf16[64,2,64,256]{3,2,1,0:T(8,128)(2,1)} async-done(((bf16[64,2,64,256]{3,2,1,0:T(8,128)(2,1)}), bf16[64,2,64,256]{3,2,1,0:T(8,128)(2,1)}, u32[]{:S(2)}, u32[]{:S(2)}) %all-to-all-start) | async-done | bytes 4194336 | tf_op jit(solution)/shard_map/all_to_all | solution.py:50
  220.2 5.4 %convolution_convert_fusion.2 = bf16[64,2,64,256]{3,2,1,0:T(8,128)(2,1)} fusion(bf16[64,2,64,256]{3,2,1,0:T(8,128)(2,1)} %all-to-all-done, bf16[1,1,256,256]{3,2,1,0:T(8,128)(2,1)S(1)} %collective-permute-done), kind=kOutput, calls=%fused_computation.2 | convolution fusion | flops 1075838976 | bytes 8519680 | tf_op jit(solution)/shard_map/scrw,wv->scrv/dot_general | solution.py:48
  225.6 0.0 copy-start
  225.7 6.2 %all-to-all-start.1 = ((bf16[64,2,64,256]{3,2,1,0:T(8,128)(2,1)}), bf16[64,2,64,256]{3,2,1,0:T(8,128)(2,1)}, u32[]{:S(2)}, u32[]{:S(2)}) async-start(bf16[64,2,64,256]{3,2,1,0:T(8,128)(2,1)} %convolution_convert_fusion.2), calls=%async_computation.1 | async-start | bytes 8388608 | tf_op jit(solution)/shard_map/all_to_all | solution.py:54
  231.9 0.0 copy-done
  231.9 0.1 copy.8
  232.0 0.1 eq.26
  232.1 189.3 %all-to-all-done.1 = bf16[64,2,64,256]{3,2,1,0:T(8,128)(2,1)} async-done(((bf16[64,2,64,256]{3,2,1,0:T(8,128)(2,1)}), bf16[64,2,64,256]{3,2,1,0:T(8,128)(2,1)}, u32[]{:S(2)}, u32[]{:S(2)}) %all-to-all-start.1) | async-done | bytes 4194336 | tf_op jit(solution)/shard_map/all_to_all | solution.py:54
  421.3 7.0 %copy.14 = bf16[16,8,64,256]{3,1,2,0:T(8,128)(2,1)} copy(bf16[16,8,64,256]{3,2,1,0:T(8,128)(2,1)} %bitcast.13) | data formatting | bytes 8388608
  428.4 3.1 convolution_convert_fusion.1
  431.4 0.8 copy.10
  (1 shorter events, 0.0 us)
Async XLA Ops:
  11.3 19.0 %copy-start.1 = (bf16[1,1,256,256]{3,2,1,0:T(8,128)(2,1)S(1)}, bf16[1,1,256,256]{3,2,1,0:T(8,128)(2,1)}, u32[]{:S(2)}) copy-start(bf16[1,1,256,256]{3,2,1,0:T(8,128)(2,1)} %param.5) | copy-start | bytes 393220
  11.3 208.9 %all-to-all-start = ((bf16[64,2,64,256]{3,2,1,0:T(8,128)(2,1)}), bf16[64,2,64,256]{3,2,1,0:T(8,128)(2,1)}, u32[]{:S(2)}, u32[]{:S(2)}) async-start(bf16[64,2,64,256]{3,2,1,0:T(8,128)(2,1)} %bitcast.21), calls=%async_computation | async-start | bytes 8388608 | tf_op jit(solution)/shard_map/all_to_all | solution.py:50
  30.3 3.2 collective-permute-start
  225.6 6.2 %copy-start = (s32[1,16,2]{1,2,0:T(2,128)S(1)}, s32[1,16,2]{1,2,0:T(2,128)}, u32[]{:S(2)}) copy-start(s32[1,16,2]{1,2,0:T(2,128)} %param.7) | copy-start | bytes 388
  225.7 195.7 %all-to-all-start.1 = ((bf16[64,2,64,256]{3,2,1,0:T(8,128)(2,1)}), bf16[64,2,64,256]{3,2,1,0:T(8,128)(2,1)}, u32[]{:S(2)}, u32[]{:S(2)}) async-start(bf16[64,2,64,256]{3,2,1,0:T(8,128)(2,1)} %convolution_convert_fusion.2), calls=%async_computation.1 | async-start | bytes 8388608 | tf_op jit(solution)/shard_map/all_to_all | solution.py:54
where the time goes:
time: 433 us; the launch traced here: 432 us
  waiting for transfers between devices  377 us (87%)
  starting transfers between devices  27.1 us (6%)
  local copies, waits for them, and re-layouts  15.6 us (4%)
  matrix products  11.9 us (3%)
    all_to_all x1, waiting for transfers between devices, per_device(): lax.all_to_all(partial_value, 'tile', split_axis=0, concat_axis=0, tiled=...  189 us
    all_to_all x1, waiting for transfers between devices, per_device(): lax.all_to_all(outbox, 'tile', split_axis=0, concat_axis=0, tiled=True)  187 us
    all_to_all x1, starting transfers between devices, per_device(): lax.all_to_all(outbox, 'tile', split_axis=0, concat_axis=0, tiled=True)  19 us
    unnamed x9, local copies, waits for them, and re-layouts  14.6 us
  transfers between devices with their start and end apart: 3, of which 3 were waited for; matrix products, arithmetic and copies ran while one was open for 0% of the time, Pallas kernels for 0%

commit v1 on v0

v1 whole, which is shorter than its diff:
```python
import functools
import jax
import jax.numpy as jnp
from jax import lax
from jax.experimental import pallas as pl
from jax.experimental.pallas import tpu as pltpu
from jax.sharding import PartitionSpec as P

RT = 8
XS = 4
META = 16

OFFSETS = (0, -5, 5, -1, -6, 4, 1, -4, 6, -2, -7, 3, 2, -3, 7, -8)


def moved(block, dz, flip=False):
    groups, tiles = lax.axis_size("irrep"), lax.axis_size("tile")
    route = []
    for g in range(groups):
        for t in range(tiles):
            to = (g ^ 1 if flip else g) * tiles + (t + dz * XS) % tiles
            route.append((g * tiles + t, to))
    return lax.ppermute(block, ("irrep", "tile"), route)


def along_x(block):
    tiles = lax.axis_size("tile")
    rows = [list(range(low, low + XS)) for low in range(0, tiles, XS)]
    return lax.all_to_all(
        block, "tile", split_axis=0, concat_axis=0, axis_index_groups=rows, tiled=True
    )


def ladder(listed, counts, amps, *refs):
    held, out, total = refs[:-2], refs[-2], refs[-1]
    rows = total.shape[1]
    own = (amps.shape[1] - META) // rows
    total[...] = jnp.zeros_like(total)
    place = 0
    for ref in held:
        for k in range(ref.shape[0]):

            def pair(q, carry, ref=ref, k=k, place=place):
                codes = [listed[place * 8 + 2 * q + i] for i in range(2)]
                tiles = []
                for code in codes:
                    tile = code >> 6
                    start = pl.multiple_of((tile % own) * rows, rows)
                    tiles.append(amps[tile // own, pl.ds(start, rows), :])
                product = jnp.dot(
                    jnp.concatenate(tiles, axis=0), ref[k], preferred_element_type=jnp.float32
                )
                for i, code in enumerate(codes):
                    total[code & 63] += product[i * rows : (i + 1) * rows]
                return carry

            pair(0, 0)
            lax.fori_loop(1, (counts[place] + 1) // 2, pair, 0)
            place += 1
    out[...] = total[: out.shape[0]].astype(out.dtype)


def per_device(amplitudes, integrals, executors, residual_slots):
    own, rows, columns = amplitudes.shape[1:]
    fanout = executors.shape[2]
    tasks = own * fanout
    depth = lax.axis_size("tile") // XS
    me = lax.axis_index("tile")
    my_x, my_z = me % XS, me // XS

    first = integrals[0]
    near = jnp.concatenate([moved(first, dz, True) for dz in (0, 5, -5)], axis=0)
    up, down = moved(near, 1), moved(near, -1)
    upper, lower = moved(up, 1), moved(down, -1)
    last = moved(up[1:2], 2)

    numbers = jnp.concatenate([executors.reshape(tasks), residual_slots.reshape(tasks)])
    meta = jnp.pad(numbers.astype(jnp.bfloat16)[None, :], ((0, META - 1), (0, columns - 2 * tasks)))
    packed = jnp.concatenate([amplitudes.reshape(own * rows, columns), meta], axis=0)
    amps = along_x(jnp.broadcast_to(packed, (XS,) + packed.shape))

    numbers = amps[:, own * rows, : 2 * tasks].astype(jnp.int32)
    target = numbers[:, :tasks].reshape(XS * tasks)
    slot = numbers[:, tasks:].reshape(XS * tasks)
    task = jnp.arange(XS * tasks, dtype=jnp.int32)
    code = (task // fanout) * 64 + (task // tasks) * RT + slot
    apart = (target // XS - my_z) % depth
    offsets = jnp.array([o % depth for o in OFFSETS], jnp.int32)
    hot = (apart[None, :] == offsets[:, None]) & (target % XS == my_x)[None, :]
    hot_bf16 = hot.astype(jnp.bfloat16)
    earlier = (task[:, None] < task[None, :]).astype(jnp.bfloat16)
    rank = jnp.dot(hot_bf16, earlier, preferred_element_type=jnp.float32).astype(jnp.int32)
    counts = jnp.sum(hot.astype(jnp.int32), axis=1)
    ranks = jnp.arange(8, dtype=jnp.int32)
    chosen = hot[:, None, :] & (rank[:, None, :] == ranks[None, :, None])
    spare = XS * RT
    listed = spare + jnp.sum(jnp.where(chosen, code - spare, 0), axis=2)

    vmem = pl.BlockSpec(memory_space=pltpu.VMEM)
    smem = pl.BlockSpec(memory_space=pltpu.SMEM)
    held = (near, up, down, upper, lower, last)
    partial = pl.pallas_call(
        ladder,
        out_shape=jax.ShapeDtypeStruct((XS * RT, rows, columns), jnp.bfloat16),
        in_specs=[smem, smem, vmem] + [vmem] * len(held),
        out_specs=vmem,
        scratch_shapes=[pltpu.VMEM((XS * RT + 1, rows, columns), jnp.float32)],
        compiler_params=pltpu.CompilerParams(vmem_limit_bytes=24 * 1024 * 1024),
        cost_estimate=pl.CostEstimate(
            flops=2 * tasks * rows * columns * columns, bytes_accessed=1 << 23, transcendentals=0
        ),
    )(listed.reshape(depth * 8), counts, amps, *held)
    back = along_x(partial).reshape(XS, RT, rows, columns)
    return jnp.sum(back.astype(jnp.float32), axis=0).astype(jnp.bfloat16)[None]


def solution(mesh):
    placed = (
        P("irrep", "tile", None, None),
        P("irrep", "tile", None, None),
        P("irrep", "tile", None),
        P("irrep", "tile", None),
    )
    return jax.shard_map(
        per_device,
        mesh=mesh,
        in_specs=placed,
        out_specs=P("irrep", "tile", None, None),
        check_vma=False,
    )
```

time: 433 us -> 106 us (0.24)
  waiting for transfers between devices: 377 us -> 30.2 us
  blocking collectives: 0 us -> 17.5 us
  starting transfers between devices: 27.1 us -> 44.1 us
  local copies, waits for them, and re-layouts: 15.6 us -> 2.92 us
  matrix products: 11.9 us -> 0.19 us
  Pallas kernels: 0 us -> 5.12 us
    all_to_all x2 -> x1, waiting for transfers between devices: 376 us -> 0.01 us  [along_x(): lax.all_to_all(block, 'tile', split_axis=0, concat_axis=0, axis_index_gro...]
    ppermute x1 -> x8, starting transfers between devices: 1.92 us -> 39.6 us  [moved(): return lax.ppermute(block, ('irrep', 'tile'), route)]
    ppermute x1 -> x8, waiting for transfers between devices: 1.31 us -> 30.2 us  [moved(): return lax.ppermute(block, ('irrep', 'tile'), route)]
    all_to_all x2 -> x1, starting transfers between devices: 25.2 us -> 4.42 us  [along_x(): lax.all_to_all(block, 'tile', split_axis=0, concat_axis=0, axis_index_gro...]
    all_to_all x0 -> x1, blocking collectives: none -> 17.5 us  [along_x(): lax.all_to_all(block, 'tile', split_axis=0, concat_axis=0, axis_index_gro...]
    unnamed x9 -> x6, local copies, waits for them, and re-layouts: 14.6 us -> 0.03 us
    dot_general x3 -> x1, matrix products: 11.9 us -> 0.19 us  [per_device(): jnp.dot(hot_bf16, earlier, preferred_element_type=jnp.float32)]
    pallas_call x0 -> x1, Pallas kernels: none -> 5.12 us  [per_device(): pl.pallas_call(ladder, out_shape=jax.ShapeDtypeStruct((XS * RT, rows, col...]
  transfers between devices with their start and end apart: 3 -> 9, of which waited for: 3 -> 5; matrix products, arithmetic and copies ran while one was open for 0% -> 2% of each run, Pallas kernels for 0% -> 0%
where the time goes in v1:
time: 106 us; the launch traced here: 104 us
  starting transfers between devices  44.1 us (42%)
  waiting for transfers between devices  30.2 us (28%)
  blocking collectives  17.5 us (17%)
  Pallas kernels  5.12 us (5%)
  other arithmetic  4.12 us (4%)
  local copies, waits for them, and re-layouts  2.92 us (3%)
    ppermute x8, starting transfers between devices, moved(): return lax.ppermute(block, ('irrep', 'tile'), route)  39.6 us
    ppermute x8, waiting for transfers between devices, moved(): return lax.ppermute(block, ('irrep', 'tile'), route)  30.2 us
    all_to_all x1, blocking collectives, along_x(): lax.all_to_all(block, 'tile', split_axis=0, concat_axis=0, axis_index_gro...  17.5 us
    pallas_call x1, Pallas kernels, per_device(): pl.pallas_call(ladder, out_shape=jax.ShapeDtypeStruct((XS * RT, rows, col...  5.12 us
    all_to_all x1, starting transfers between devices, along_x(): lax.all_to_all(block, 'tile', split_axis=0, concat_axis=0, axis_index_gro...  4.42 us
  transfers between devices with their start and end apart: 9, of which 5 were waited for; matrix products, arithmetic and copies ran while one was open for 2% of the time, Pallas kernels for 0%

profile of v1, /device:TPU:24, one launch (start us, length us, event | category | flops | bytes accessed | tf_op | source)
XLA Modules:
  0.0 104.3 jit_solution(13251001368269718539)
XLA Ops:
  0.0 0.7 convert.10
  0.7 0.1 copy.10
  0.8 0.1 concatenate.21
  0.9 0.7 convert.11
  1.6 0.1 copy.11
  1.7 0.1 concatenate.22
  1.8 0.1 fusion.6
  1.8 1.1 %pad_maximum_fusion = bf16[1040,256]{1,0:T(8,128)(2,1)S(1)} fusion(bf16[16,256]{1,0:T(8,128)(2,1)S(1)} %fusion.6, bf16[1024,256]{1,0:T(8,128)(2,1)} %bitcast.6), kind=kLoop, calls=%fused_computation.1 | loop fusion | flops 1064960 | bytes 1064960 | tf_op jit(solution)/shard_map/concatenate | solution.py:79
  2.9 1.5 %broadcast_in_dim.10 = bf16[4,1040,256]{2,1,0:T(8,128)(2,1)} broadcast(bf16[1040,256]{1,0:T(8,128)(2,1)S(1)} %pad_maximum_fusion), dimensions={1,2} | broadcast | bytes 2662400 | tf_op jit(solution)/shard_map/broadcast_in_dim | solution.py:80
  4.4 0.0 copy-start.1
  4.4 0.0 copy-start
  4.4 4.4 %all-to-all-start = ((bf16[4,1040,256]{2,1,0:T(8,128)(2,1)}), bf16[4,1040,256]{2,1,0:T(8,128)(2,1)S(1)}, u32[]{:S(2)}, u32[]{:S(2)}) async-start(bf16[4,1040,256]{2,1,0:T(8,128)(2,1)} %broadcast_in_dim.10), calls=%async_computation | async-start | bytes 4259840 | tf_op jit(solution)/shard_map/all_to_all | solution.py:29
  8.9 0.0 copy-done.1
  8.9 1.9 %collective-permute-start = (bf16[1,256,256]{2,1,0:T(8,128)(2,1)S(1)}, bf16[1,256,256]{2,1,0:T(8,128)(2,1)S(1)}, u32[]{:S(2)}, u32[]{:S(2)}) collective-permute-start(bf16[1,256,256]{2,1,0:T(8,128)(2,1)S(1)} %bitcast.8), channel_id=1, source_target_pairs={{0,64},{1,65},{2,66},{3,67},{4,68},{5,69},{6,70},{7,71},{8,72},{9,... | collective-permute-start | bytes 393224 | tf_op jit(solution)/shard_map/ppermute | solution.py:23
  10.8 10.6 %collective-permute-start.1 = (bf16[1,256,256]{2,1,0:T(8,128)(2,1)S(1)}, bf16[1,256,256]{2,1,0:T(8,128)(2,1)S(1)}, u32[]{:S(2)}, u32[]{:S(2)}) collective-permute-start(bf16[1,256,256]{2,1,0:T(8,128)(2,1)S(1)} %bitcast.9), channel_id=1, source_target_pairs={{0,84},{1,85},{2,86},{3,87},{4,88},{5,89},{6,90},{7,91},{8,92},{9,... | collective-permute-start | bytes 393224 | tf_op jit(solution)/shard_map/ppermute | solution.py:23
  21.3 5.9 %collective-permute-start.2 = (bf16[1,256,256]{2,1,0:T(8,128)(2,1)S(1)}, bf16[1,256,256]{2,1,0:T(8,128)(2,1)S(1)}, u32[]{:S(2)}, u32[]{:S(2)}) collective-permute-start(bf16[1,256,256]{2,1,0:T(8,128)(2,1)S(1)} %bitcast.10), channel_id=1, source_target_pairs={{0,108},{1,109},{2,110},{3,111},{4,112},{5,113},{6,114},{7,115},{8... | collective-permute-start | bytes 393224 | tf_op jit(solution)/shard_map/ppermute | solution.py:23
  27.2 0.0 collective-permute-done
  27.2 2.2 %collective-permute-done.1 = bf16[1,256,256]{2,1,0:T(8,128)(2,1)S(1)} collective-permute-done((bf16[1,256,256]{2,1,0:T(8,128)(2,1)S(1)}, bf16[1,256,256]{2,1,0:T(8,128)(2,1)S(1)}, u32[]{:S(2)}, u32[]{:S(2)}) %collective-permute-start.1) | collective-permute-done | bytes 131104 | tf_op jit(solution)/shard_map/ppermute | solution.py:23
  29.5 12.7 %collective-permute-done.2 = bf16[1,256,256]{2,1,0:T(8,128)(2,1)S(1)} collective-permute-done((bf16[1,256,256]{2,1,0:T(8,128)(2,1)S(1)}, bf16[1,256,256]{2,1,0:T(8,128)(2,1)S(1)}, u32[]{:S(2)}, u32[]{:S(2)}) %collective-permute-start.2) | collective-permute-done | bytes 131104 | tf_op jit(solution)/shard_map/ppermute | solution.py:23
  42.2 2.0 %collective-permute-start.3 = (bf16[3,256,256]{2,1,0:T(8,128)(2,1)S(1)}, bf16[3,256,256]{2,1,0:T(8,128)(2,1)S(1)}, u32[]{:S(2)}, u32[]{:S(2)}) collective-permute-start(bf16[3,256,256]{2,1,0:T(8,128)(2,1)S(1)} %constant_dynamic-update-slice_fusion.refs_0_), channel_id=1, source_target_pairs={{0,4},{1,5},{2,6},{3,7},{4,8},{5,9},{6,10},{7,11},{8,12},{9,13},{1... | collective-permute-start | bytes 1179656 | tf_op jit(solution)/shard_map/ppermute | solution.py:23
  44.2 5.7 %collective-permute-start.4 = (bf16[3,256,256]{2,1,0:T(8,128)(2,1)S(1)}, bf16[3,256,256]{2,1,0:T(8,128)(2,1)S(1)}, u32[]{:S(2)}, u32[]{:S(2)}) collective-permute-start(bf16[3,256,256]{2,1,0:T(8,128)(2,1)S(1)} %constant_dynamic-update-slice_fusion.refs_0_), channel_id=1, source_target_pairs={{0,60},{1,61},{2,62},{3,63},{4,0},{5,1},{6,2},{7,3},{8,4},{9,5},{1... | collective-permute-start | bytes 1179656 | tf_op jit(solution)/shard_map/ppermute | solution.py:23
  50.0 7.4 %collective-permute-done.3.refs_1_ = bf16[3,256,256]{2,1,0:T(8,128)(2,1)S(1)} collective-permute-done((bf16[3,256,256]{2,1,0:T(8,128)(2,1)S(1)}, bf16[3,256,256]{2,1,0:T(8,128)(2,1)S(1)}, u32[]{:S(2)}, u32[]{:S(2)}) %collective-permute-start.3) | collective-permute-done | bytes 393248 | tf_op jit(solution)/shard_map/ppermute | solution.py:23
  57.3 0.7 slice.17
  58.0 6.5 %collective-permute-start.7 = (bf16[1,256,256]{2,1,0:T(8,128)(2,1)}, bf16[1,256,256]{2,1,0:T(8,128)(2,1)S(1)}, u32[]{:S(2)}, u32[]{:S(2)}) collective-permute-start(bf16[1,256,256]{2,1,0:T(8,128)(2,1)} %slice.17), channel_id=1, source_target_pairs={{0,8},{1,9},{2,10},{3,11},{4,12},{5,13},{6,14},{7,15},{8,16},{9,17... | collective-permute-start | bytes 393224 | tf_op jit(solution)/shard_map/ppermute | solution.py:23
  64.5 4.4 %collective-permute-start.5 = (bf16[3,256,256]{2,1,0:T(8,128)(2,1)S(1)}, bf16[3,256,256]{2,1,0:T(8,128)(2,1)}, u32[]{:S(2)}, u32[]{:S(2)}) collective-permute-start(bf16[3,256,256]{2,1,0:T(8,128)(2,1)S(1)} %collective-permute-done.3.refs_1_), channel_id=1, source_target_pairs={{0,4},{1,5},{2,6},{3,7},{4,8},{5,9},{6,10},{7,11},{8,12},{9,13},{1... | collective-permute-start | bytes 1179656 | tf_op jit(solution)/shard_map/ppermute | solution.py:23
  68.9 0.0 collective-permute-done.4.refs_2_
  68.9 2.7 %collective-permute-start.6 = (bf16[3,256,256]{2,1,0:T(8,128)(2,1)S(1)}, bf16[3,256,256]{2,1,0:T(8,128)(2,1)}, u32[]{:S(2)}, u32[]{:S(2)}) collective-permute-start(bf16[3,256,256]{2,1,0:T(8,128)(2,1)S(1)} %collective-permute-done.4.refs_2_), channel_id=1, source_target_pairs={{0,60},{1,61},{2,62},{3,63},{4,0},{5,1},{6,2},{7,3},{8,4},{9,5},{1... | collective-permute-start | bytes 1179656 | tf_op jit(solution)/shard_map/ppermute | solution.py:23
  71.6 0.0 all-to-all-done.amps
  71.6 0.1 fusion.14
  71.7 0.1 reshape.152
  71.8 0.0 copy-done
  71.8 0.1 compare_and_fusion
  71.9 0.2 convolution_convert_fusion
  72.1 0.1 reshape.153
  72.2 0.4 select_reduce_fusion
  72.6 0.1 add.56.listed
  72.7 0.2 convert_reduce_fusion.counts
  72.8 0.0 collective-permute-done.7.refs_5_
  72.8 5.8 %collective-permute-done.5.refs_3_ = bf16[3,256,256]{2,1,0:T(8,128)(2,1)} collective-permute-done((bf16[3,256,256]{2,1,0:T(8,128)(2,1)S(1)}, bf16[3,256,256]{2,1,0:T(8,128)(2,1)}, u32[]{:S(2)}, u32[]{:S(2)}) %collective-permute-start.5) | collective-permute-done | bytes 393248 | tf_op jit(solution)/shard_map/ppermute | solution.py:23
  78.6 2.1 %collective-permute-done.6.refs_4_ = bf16[3,256,256]{2,1,0:T(8,128)(2,1)} collective-permute-done((bf16[3,256,256]{2,1,0:T(8,128)(2,1)S(1)}, bf16[3,256,256]{2,1,0:T(8,128)(2,1)}, u32[]{:S(2)}, u32[]{:S(2)}) %collective-permute-start.6) | collective-permute-done | bytes 393248 | tf_op jit(solution)/shard_map/ppermute | solution.py:23
  80.7 5.1 %shard_map.55 = bf16[32,64,256]{2,1,0:T(8,128)(2,1)S(1)} custom-call(s32[128]{0:T(128)S(1)} %add.56.listed, s32[16]{0:T(128)S(1)} %convert_reduce_fusion.counts, bf16[4,1040,256]{2,1,0:T(8,128)(2,1)S(1)} %all-to-all-done.amps, bf16[3,256,256]{2,1,0:T(8,128)(2,1)S(1)} %constant_dynamic-update-slice_fusion.refs_0_, ...), custom_call_target="tpu_custom_call" | custom-call | flops 268435456 | bytes 8388608 | tf_op jit(solution)/shard_map/pallas_call | solution.py:102
  85.8 17.5 %all_to_all.10 = bf16[32,64,256]{2,1,0:T(8,128)(2,1)S(1)} all-to-all(bf16[32,64,256]{2,1,0:T(8,128)(2,1)S(1)} %shard_map.55), channel_id=1, replica_groups={{0,1,2,3},{4,5,6,7},{8,9,10,11},{12,13,14,15},{16,17,18,19},{20,21,22,2..., dimensions={0} | all-to-all | bytes 2097152 | tf_op jit(solution)/shard_map/all_to_all | solution.py:29
  103.4 0.9 reduce_sum.32
  (8 shorter events, 0.1 us)
Async XLA Ops:
  4.4 4.4 %copy-start.1 = (bf16[1,1,256,256]{3,2,1,0:T(8,128)(2,1)S(1)}, bf16[1,1,256,256]{3,2,1,0:T(8,128)(2,1)}, u32[]{:S(2)}) copy-start(bf16[1,1,256,256]{3,2,1,0:T(8,128)(2,1)} %param.6) | copy-start | bytes 393220
  4.4 67.4 %copy-start = (s32[16]{0:T(128)S(1)}, s32[16]{0:T(128)}, u32[]{:S(2)}) copy-start(s32[16]{0:T(128)} %constant.98.clone) | copy-start | bytes 196
  4.4 67.2 %all-to-all-start = ((bf16[4,1040,256]{2,1,0:T(8,128)(2,1)}), bf16[4,1040,256]{2,1,0:T(8,128)(2,1)S(1)}, u32[]{:S(2)}, u32[]{:S(2)}) async-start(bf16[4,1040,256]{2,1,0:T(8,128)(2,1)} %broadcast_in_dim.10), calls=%async_computation | async-start | bytes 4259840 | tf_op jit(solution)/shard_map/all_to_all | solution.py:29
  8.9 18.3 %collective-permute-start = (bf16[1,256,256]{2,1,0:T(8,128)(2,1)S(1)}, bf16[1,256,256]{2,1,0:T(8,128)(2,1)S(1)}, u32[]{:S(2)}, u32[]{:S(2)}) collective-permute-start(bf16[1,256,256]{2,1,0:T(8,128)(2,1)S(1)} %bitcast.8), channel_id=1, source_target_pairs={{0,64},{1,65},{2,66},{3,67},{4,68},{5,69},{6,70},{7,71},{8,72},{9,... | collective-permute-start | bytes 393224 | tf_op jit(solution)/shard_map/ppermute | solution.py:23
  10.8 18.7 %collective-permute-start.1 = (bf16[1,256,256]{2,1,0:T(8,128)(2,1)S(1)}, bf16[1,256,256]{2,1,0:T(8,128)(2,1)S(1)}, u32[]{:S(2)}, u32[]{:S(2)}) collective-permute-start(bf16[1,256,256]{2,1,0:T(8,128)(2,1)S(1)} %bitcast.9), channel_id=1, source_target_pairs={{0,84},{1,85},{2,86},{3,87},{4,88},{5,89},{6,90},{7,91},{8,92},{9,... | collective-permute-start | bytes 393224 | tf_op jit(solution)/shard_map/ppermute | solution.py:23
  21.3 20.8 %collective-permute-start.2 = (bf16[1,256,256]{2,1,0:T(8,128)(2,1)S(1)}, bf16[1,256,256]{2,1,0:T(8,128)(2,1)S(1)}, u32[]{:S(2)}, u32[]{:S(2)}) collective-permute-start(bf16[1,256,256]{2,1,0:T(8,128)(2,1)S(1)} %bitcast.10), channel_id=1, source_target_pairs={{0,108},{1,109},{2,110},{3,111},{4,112},{5,113},{6,114},{7,115},{8... | collective-permute-start | bytes 393224 | tf_op jit(solution)/shard_map/ppermute | solution.py:23
  42.2 15.1 %collective-permute-start.3 = (bf16[3,256,256]{2,1,0:T(8,128)(2,1)S(1)}, bf16[3,256,256]{2,1,0:T(8,128)(2,1)S(1)}, u32[]{:S(2)}, u32[]{:S(2)}) collective-permute-start(bf16[3,256,256]{2,1,0:T(8,128)(2,1)S(1)} %constant_dynamic-update-slice_fusion.refs_0_), channel_id=1, source_target_pairs={{0,4},{1,5},{2,6},{3,7},{4,8},{5,9},{6,10},{7,11},{8,12},{9,13},{1... | collective-permute-start | bytes 1179656 | tf_op jit(solution)/shard_map/ppermute | solution.py:23
  44.2 24.7 %collective-permute-start.4 = (bf16[3,256,256]{2,1,0:T(8,128)(2,1)S(1)}, bf16[3,256,256]{2,1,0:T(8,128)(2,1)S(1)}, u32[]{:S(2)}, u32[]{:S(2)}) collective-permute-start(bf16[3,256,256]{2,1,0:T(8,128)(2,1)S(1)} %constant_dynamic-update-slice_fusion.refs_0_), channel_id=1, source_target_pairs={{0,60},{1,61},{2,62},{3,63},{4,0},{5,1},{6,2},{7,3},{8,4},{9,5},{1... | collective-permute-start | bytes 1179656 | tf_op jit(solution)/shard_map/ppermute | solution.py:23
  58.0 14.8 %collective-permute-start.7 = (bf16[1,256,256]{2,1,0:T(8,128)(2,1)}, bf16[1,256,256]{2,1,0:T(8,128)(2,1)S(1)}, u32[]{:S(2)}, u32[]{:S(2)}) collective-permute-start(bf16[1,256,256]{2,1,0:T(8,128)(2,1)} %slice.17), channel_id=1, source_target_pairs={{0,8},{1,9},{2,10},{3,11},{4,12},{5,13},{6,14},{7,15},{8,16},{9,17... | collective-permute-start | bytes 393224 | tf_op jit(solution)/shard_map/ppermute | solution.py:23
  64.5 14.1 %collective-permute-start.5 = (bf16[3,256,256]{2,1,0:T(8,128)(2,1)S(1)}, bf16[3,256,256]{2,1,0:T(8,128)(2,1)}, u32[]{:S(2)}, u32[]{:S(2)}) collective-permute-start(bf16[3,256,256]{2,1,0:T(8,128)(2,1)S(1)} %collective-permute-done.3.refs_1_), channel_id=1, source_target_pairs={{0,4},{1,5},{2,6},{3,7},{4,8},{5,9},{6,10},{7,11},{8,12},{9,13},{1... | collective-permute-start | bytes 1179656 | tf_op jit(solution)/shard_map/ppermute | solution.py:23
  68.9 11.8 %collective-permute-start.6 = (bf16[3,256,256]{2,1,0:T(8,128)(2,1)S(1)}, bf16[3,256,256]{2,1,0:T(8,128)(2,1)}, u32[]{:S(2)}, u32[]{:S(2)}) collective-permute-start(bf16[3,256,256]{2,1,0:T(8,128)(2,1)S(1)} %collective-permute-done.4.refs_2_), channel_id=1, source_target_pairs={{0,60},{1,61},{2,62},{3,63},{4,0},{5,1},{6,2},{7,3},{8,4},{9,5},{1... | collective-permute-start | bytes 1179656 | tf_op jit(solution)/shard_map/ppermute | solution.py:23

commit v2 on v1

v2 whole, which is shorter than its diff:
```python
import functools
import jax
import jax.numpy as jnp
from jax import lax
from jax.experimental import pallas as pl
from jax.experimental.pallas import tpu as pltpu
from jax.sharding import PartitionSpec as P

RT = 8
XS = 4
SKIP = 4

META = 16

APART = (0,) * 4 + (-1,) * 4 + (1,) * 4 + (2,) * 4


def moved(block, dz, flip=False):
    groups, tiles = lax.axis_size("irrep"), lax.axis_size("tile")
    route = []
    for g in range(groups):
        for t in range(tiles):
            to = (g ^ 1 if flip else g) * tiles + (t + dz * XS) % tiles
            route.append((g * tiles + t, to))
    return lax.ppermute(block, ("irrep", "tile"), route)


def along_x(block):
    tiles = lax.axis_size("tile")
    rows = [list(range(low, low + XS)) for low in range(0, tiles, XS)]
    return lax.all_to_all(
        block, "tile", split_axis=0, concat_axis=0, axis_index_groups=rows, tiled=True
    )


def every_fourth(block):
    tiles = lax.axis_size("tile")
    step = SKIP * XS
    groups = [list(range(low, tiles, step)) for low in range(step)]
    return lax.all_gather(block, "tile", axis=0, axis_index_groups=groups, tiled=True)


def pack(amps, targets, slots, out, meta, sems):
    size, (fanout, count) = amps.shape[0], targets.shape
    copies = [
        pltpu.make_async_copy(amps, out.at[x, pl.ds(0, size)], sems.at[x]) for x in range(XS)
    ]
    for copy in copies:
        copy.start()
    numbers = jnp.concatenate([targets[...], slots[...]], axis=0).astype(jnp.float32)
    numbers = jnp.pad(numbers, ((0, meta.shape[0] - 2 * fanout), (0, meta.shape[1] - count)))
    meta[...] = numbers.astype(meta.dtype)
    for x in range(XS):
        copies.append(
            pltpu.make_async_copy(
                meta, out.at[x, pl.ds(size, meta.shape[0])], sems.at[XS + x]
            )
        )
        copies[-1].start()
    for copy in copies:
        copy.wait()


def ladder(first, listed, counts, amps, *refs):
    held, out, total = refs[:-2], refs[-2], refs[-1]
    rows = total.shape[1]
    own = (amps.shape[1] - META) // rows
    if first:
        total[...] = held[0][...]
        held = held[1:]
    else:
        total[...] = jnp.zeros_like(total)
    place = first
    for ref in held:
        for k in range(ref.shape[0]):

            def pair(q, carry, ref=ref, k=k, place=place):
                codes = [listed[place * 8 + 2 * q + i] for i in range(2)]
                tiles = []
                for code in codes:
                    tile = code >> 6
                    start = pl.multiple_of((tile % own) * rows, rows)
                    tiles.append(amps[tile // own, pl.ds(start, rows), :])
                product = jnp.dot(
                    jnp.concatenate(tiles, axis=0), ref[k], preferred_element_type=jnp.float32
                )
                for i, code in enumerate(codes):
                    total[code & 63] += product[i * rows : (i + 1) * rows]
                return carry

            pair(0, 0)
            lax.fori_loop(1, (counts[place] + 1) // 2, pair, 0)
            place += 1
    out[...] = total[: out.shape[0]].astype(out.dtype)


def multiply(first, listed, counts, amps, held, out_shape, out_dtype):
    vmem = pl.BlockSpec(memory_space=pltpu.VMEM)
    smem = pl.BlockSpec(memory_space=pltpu.SMEM)
    rows, columns = held[-1].shape[-2] // 4, held[-1].shape[-1]
    spare_shape = (XS * RT + 1, rows, columns)
    return pl.pallas_call(
        functools.partial(ladder, first),
        out_shape=jax.ShapeDtypeStruct(out_shape, out_dtype),
        in_specs=[smem, smem, vmem] + [vmem] * len(held),
        out_specs=vmem,
        scratch_shapes=[pltpu.VMEM(spare_shape, jnp.float32)],
        compiler_params=pltpu.CompilerParams(vmem_limit_bytes=24 * 1024 * 1024),
        cost_estimate=pl.CostEstimate(
            flops=1 << 28, bytes_accessed=1 << 23, transcendentals=0
        ),
    )(listed, counts, amps, *held)


def per_device(amplitudes, integrals, executors, residual_slots):
    own, rows, columns = amplitudes.shape[1:]
    fanout = executors.shape[2]
    tasks = own * fanout
    depth = lax.axis_size("tile") // XS
    me = lax.axis_index("tile")
    my_x, my_z = me % XS, me // XS

    vmem = pl.BlockSpec(memory_space=pltpu.VMEM)
    anywhere = pl.BlockSpec(memory_space=pl.ANY)
    flat = own * rows
    packed = pl.pallas_call(
        pack,
        out_shape=jax.ShapeDtypeStruct((XS, flat + META, columns), jnp.bfloat16),
        in_specs=[vmem, vmem, vmem],
        out_specs=anywhere,
        scratch_shapes=[
            pltpu.VMEM((META, columns), jnp.bfloat16),
            pltpu.SemaphoreType.DMA((2 * XS,)),
        ],
    )(amplitudes.reshape(flat, columns), executors[0].T, residual_slots[0].T)
    integrals, packed = lax.optimization_barrier((integrals, packed))
    amps = along_x(packed)
    mine = every_fourth(integrals[0])
    mine, amps = lax.optimization_barrier((mine, amps))
    near, up, down = moved(mine, 0, True), moved(mine, 1, True), moved(mine, -1, True)
    upper, lower = moved(up[:2], 1), moved(down[2:], -1)

    numbers = amps[:, flat : flat + 2 * fanout, :own].astype(jnp.int32)
    target = numbers[:, :fanout].reshape(XS * tasks)
    slot = numbers[:, fanout:].reshape(XS * tasks)
    task = jnp.arange(XS * tasks, dtype=jnp.int32)
    source = task // tasks
    code = (source * own + task % own) * 64 + source * RT + slot
    place = jnp.arange(depth, dtype=jnp.int32)
    place_z = (my_z + jnp.array(APART, jnp.int32)) % SKIP + SKIP * (place % SKIP)
    hot = target[None, :] == (place_z * XS + my_x)[:, None]
    hot_bf16 = hot.astype(jnp.bfloat16)
    earlier = (task[:, None] < task[None, :]).astype(jnp.bfloat16)
    rank = jnp.dot(hot_bf16, earlier, preferred_element_type=jnp.float32).astype(jnp.int32)
    counts = jnp.sum(hot.astype(jnp.int32), axis=1)
    ranks = jnp.arange(8, dtype=jnp.int32)
    chosen = hot[:, None, :] & (rank[:, None, :] == ranks[None, :, None])
    spare = XS * RT
    listed = spare + jnp.sum(jnp.where(chosen, code - spare, 0), axis=2)
    listed = listed.reshape(depth * 8)

    total = multiply(
        0, listed, counts, amps, (near, up, down), (spare + 1, rows, columns), jnp.float32
    )
    partial = multiply(
        12, listed, counts, amps, (total, upper, lower), (spare, rows, columns), jnp.bfloat16
    )
    back = along_x(partial).reshape(XS, RT, rows, columns)
    return jnp.sum(back.astype(jnp.float32), axis=0).astype(jnp.bfloat16)[None]


def solution(mesh):
    placed = (
        P("irrep", "tile", None, None),
        P("irrep", "tile", None, None),
        P("irrep", "tile", None),
        P("irrep", "tile", None),
    )
    return jax.shard_map(
        per_device,
        mesh=mesh,
        in_specs=placed,
        out_specs=P("irrep", "tile", None, None),
        check_vma=False,
    )
```

time: 106 us -> 94.1 us (0.89)
  blocking collectives: 17.5 us -> 54.2 us
  starting transfers between devices: 44.1 us -> 20.2 us
  waiting for transfers between devices: 30.2 us -> 7.17 us
  Pallas kernels: 5.12 us -> 8.27 us
  other arithmetic: 4.12 us -> 1.56 us
  local copies, waits for them, and re-layouts: 2.92 us -> 1.7 us
    all_gather x0 -> x1, blocking collectives: none -> 34.9 us  [every_fourth(): lax.all_gather(block, 'tile', axis=0, axis_index_groups=groups, tiled=True)]
    ppermute x8 -> x5, starting transfers between devices: 39.6 us -> 15.7 us  [moved(): return lax.ppermute(block, ('irrep', 'tile'), route)]
    ppermute x8 -> x5, waiting for transfers between devices: 30.2 us -> 7.17 us  [moved(): return lax.ppermute(block, ('irrep', 'tile'), route)]
    pallas_call x1 -> x3, Pallas kernels: 5.12 us -> 8.27 us  [the longest x2 5.8 us: multiply(): pl.pallas_call(functools.partial(ladder, first), out_shape=jax.ShapeDtype...]
    all_to_all x1, blocking collectives: 17.5 us -> 19.4 us  [along_x(): lax.all_to_all(block, 'tile', split_axis=0, concat_axis=0, axis_index_gro...]
    broadcast_in_dim x1 -> x0, local copies, waits for them, and re-layouts: 1.5 us -> none  [per_device(): amps = along_x(jnp.broadcast_to(packed, (XS,) + packed.shape))]
    another operation x2 -> x0, other arithmetic: 1.37 us -> none
    concatenate x2 -> x0, other arithmetic: 1.16 us -> none  [the longest x1 1.08 us: per_device(): jnp.concatenate([amplitudes.reshape(own * rows, columns), meta], axis=0)]
  transfers between devices with their start and end apart: 9 -> 6, of which waited for: 5 -> 2; matrix products, arithmetic and copies ran while one was open for 2% -> 3% of each run, Pallas kernels for 0% -> 4%
where the time goes in v2:
time: 94.1 us; the launch traced here: 93.4 us
  blocking collectives  54.2 us (58%)
  starting transfers between devices  20.2 us (21%)
  Pallas kernels  8.27 us (9%)
  waiting for transfers between devices  7.17 us (8%)
  local copies, waits for them, and re-layouts  1.7 us (2%)
  other arithmetic  1.56 us (2%)
    all_gather x1, blocking collectives, every_fourth(): lax.all_gather(block, 'tile', axis=0, axis_index_groups=groups, tiled=True)  34.9 us
    all_to_all x1, blocking collectives, along_x(): lax.all_to_all(block, 'tile', split_axis=0, concat_axis=0, axis_index_gro...  19.4 us
    ppermute x5, starting transfers between devices, moved(): return lax.ppermute(block, ('irrep', 'tile'), route)  15.7 us
    ppermute x5, waiting for transfers between devices, moved(): return lax.ppermute(block, ('irrep', 'tile'), route)  7.17 us
    pallas_call x2, Pallas kernels, multiply(): pl.pallas_call(functools.partial(ladder, first), out_shape=jax.ShapeDtype...  5.8 us
    all_to_all x1, starting transfers between devices, along_x(): lax.all_to_all(block, 'tile', split_axis=0, concat_axis=0, axis_index_gro...  4.44 us
    pallas_call x1, Pallas kernels, per_device(): pl.pallas_call(pack, out_shape=jax.ShapeDtypeStruct((XS, flat + META, col...  2.46 us
  transfers between devices with their start and end apart: 6, of which 2 were waited for; matrix products, arithmetic and copies ran while one was open for 3% of the time, Pallas kernels for 4%

profile of v2, /device:TPU:24, one launch (start us, length us, event | category | flops | bytes accessed | tf_op | source)
XLA Modules:
  0.0 93.4 jit_solution(16963389058683533068)
XLA Ops:
  0.0 2.5 %shard_map.55 = bf16[4,1040,256]{2,1,0:T(8,128)(2,1)} custom-call(bf16[1024,256]{1,0:T(8,128)(2,1)} %bitcast.11, s32[2,16]{1,0:T(2,128)} %bitcast.12, s32[2,16]{1,0:T(2,128)} %bitcast.13), custom_call_target="tpu_custom_call" | custom-call | tf_op jit(solution)/shard_map/pallas_call | solution.py:126
  2.5 0.0 copy-start
  2.5 0.0 copy-start.1
  2.5 4.4 %all-to-all-start = ((bf16[4,1040,256]{2,1,0:T(8,128)(2,1)}), bf16[4,1040,256]{2,1,0:T(8,128)(2,1)S(1)}, u32[]{:S(2)}, u32[]{:S(2)}) async-start(bf16[4,1040,256]{2,1,0:T(8,128)(2,1)} %shard_map.55), calls=%async_computation | async-start | bytes 4259840 | tf_op jit(solution)/shard_map/all_to_all | solution.py:31
  6.9 0.0 copy-done
  6.9 34.9 %all-gather = bf16[4,1,256,256]{3,2,1,0:T(8,128)(2,1)} all-gather(bf16[1,1,256,256]{3,2,1,0:T(8,128)(2,1)S(1)} %copy-done), channel_id=2, replica_groups={{0,16,32,48},{1,17,33,49},{2,18,34,50},{3,19,35,51},{4,20,36,52},{5,21,..., dimensions={0}, use_global_device_ids=true | all-gather | bytes 655360 | tf_op jit(solution)/shard_map/all_gather | solution.py:40
  41.8 0.0 copy-done.1
  41.8 0.0 all-to-all-done.amps
  41.8 1.9 %collective-permute-start.1 = (bf16[4,256,256]{2,1,0:T(8,128)(2,1)}, bf16[4,256,256]{2,1,0:T(8,128)(2,1)S(1)}, u32[]{:S(2)}, u32[]{:S(2)}) collective-permute-start(bf16[4,256,256]{2,1,0:T(8,128)(2,1)} %bitcast.5), channel_id=1, source_target_pairs={{0,68},{1,69},{2,70},{3,71},{4,72},{5,73},{6,74},{7,75},{8,76},{9,... | collective-permute-start | bytes 1572872 | tf_op jit(solution)/shard_map/ppermute | solution.py:25
  43.7 4.9 %collective-permute-start.2 = (bf16[4,256,256]{2,1,0:T(8,128)(2,1)}, bf16[4,256,256]{2,1,0:T(8,128)(2,1)S(1)}, u32[]{:S(2)}, u32[]{:S(2)}) collective-permute-start(bf16[4,256,256]{2,1,0:T(8,128)(2,1)} %bitcast.5), channel_id=1, source_target_pairs={{0,124},{1,125},{2,126},{3,127},{4,64},{5,65},{6,66},{7,67},{8,68}... | collective-permute-start | bytes 1572872 | tf_op jit(solution)/shard_map/ppermute | solution.py:25
  48.6 1.9 %collective-permute-start = (bf16[4,256,256]{2,1,0:T(8,128)(2,1)}, bf16[4,256,256]{2,1,0:T(8,128)(2,1)}, u32[]{:S(2)}, u32[]{:S(2)}) collective-permute-start(bf16[4,256,256]{2,1,0:T(8,128)(2,1)} %bitcast.5), channel_id=1, source_target_pairs={{0,64},{1,65},{2,66},{3,67},{4,68},{5,69},{6,70},{7,71},{8,72},{9,... | collective-permute-start | bytes 1572872 | tf_op jit(solution)/shard_map/ppermute | solution.py:25
  50.6 0.1 eq.39
  50.6 0.1 reshape.41
  50.7 0.2 convolution_convert_fusion
  50.9 0.1 broadcast_compare_fusion
  51.0 0.3 select_reduce_fusion
  51.4 6.6 %collective-permute-done.1.refs_1_ = bf16[4,256,256]{2,1,0:T(8,128)(2,1)S(1)} collective-permute-done((bf16[4,256,256]{2,1,0:T(8,128)(2,1)}, bf16[4,256,256]{2,1,0:T(8,128)(2,1)S(1)}, u32[]{:S(2)}, u32[]{:S(2)}) %collective-permute-start.1) | collective-permute-done | bytes 524320 | tf_op jit(solution)/shard_map/ppermute | solution.py:25
  58.0 0.7 slice.22
  58.7 1.9 %collective-permute-start.3 = (bf16[2,256,256]{2,1,0:T(8,128)(2,1)}, bf16[2,256,256]{2,1,0:T(8,128)(2,1)S(1)}, u32[]{:S(2)}, u32[]{:S(2)}) collective-permute-start(bf16[2,256,256]{2,1,0:T(8,128)(2,1)} %slice.22), channel_id=1, source_target_pairs={{0,4},{1,5},{2,6},{3,7},{4,8},{5,9},{6,10},{7,11},{8,12},{9,13},{1... | collective-permute-start | bytes 786440 | tf_op jit(solution)/shard_map/ppermute | solution.py:25
  60.6 0.0 collective-permute-done.2.refs_2_
  60.6 0.7 slice.23
  61.3 5.1 %collective-permute-start.4 = (bf16[2,256,256]{2,1,0:T(8,128)(2,1)}, bf16[2,256,256]{2,1,0:T(8,128)(2,1)}, u32[]{:S(2)}, u32[]{:S(2)}) collective-permute-start(bf16[2,256,256]{2,1,0:T(8,128)(2,1)} %slice.23), channel_id=1, source_target_pairs={{0,60},{1,61},{2,62},{3,63},{4,0},{5,1},{6,2},{7,3},{8,4},{9,5},{1... | collective-permute-start | bytes 786440 | tf_op jit(solution)/shard_map/ppermute | solution.py:25
  66.5 0.1 add.71.listed
  66.6 0.2 convert_reduce_fusion.counts
  66.7 0.0 collective-permute-done.refs_0_
  66.8 3.9 %shard_map.56.refs_0_ = f32[33,64,256]{2,1,0:T(8,128)S(1)} custom-call(s32[128]{0:T(128)S(1)} %add.71.listed, s32[16]{0:T(128)S(1)} %convert_reduce_fusion.counts, bf16[4,1040,256]{2,1,0:T(8,128)(2,1)S(1)} %all-to-all-done.amps, bf16[4,256,256]{2,1,0:T(8,128)(2,1)} %collective-permute-done.refs_0_, bf16[4,256,256]{2,1,0:T(8,128)(2,1)S(1)} %collective-permute-done.1.refs_1_, ...), custom_call_target="tpu_custom_call" | custom-call | flops 268435456 | bytes 8388608 | tf_op jit(solution)/shard_map/pallas_call | solution.py:102
  70.6 0.0 collective-permute-done.3.refs_1_
  70.6 0.5 collective-permute-done.4.refs_2_
  71.2 2.0 %shard_map.57 = bf16[32,64,256]{2,1,0:T(8,128)(2,1)S(1)} custom-call(s32[128]{0:T(128)S(1)} %add.71.listed, s32[16]{0:T(128)S(1)} %convert_reduce_fusion.counts, bf16[4,1040,256]{2,1,0:T(8,128)(2,1)S(1)} %all-to-all-done.amps, f32[33,64,256]{2,1,0:T(8,128)S(1)} %shard_map.56.refs_0_, bf16[2,256,256]{2,1,0:T(8,128)(2,1)S(1)} %collective-permute-done.3.refs_1_, ...), custom_call_target="tpu_custom_call" | custom-call | flops 268435456 | bytes 8388608 | tf_op jit(solution)/shard_map/pallas_call | solution.py:102
  73.1 19.4 %all_to_all.10 = bf16[32,64,256]{2,1,0:T(8,128)(2,1)S(1)} all-to-all(bf16[32,64,256]{2,1,0:T(8,128)(2,1)S(1)} %shard_map.57), channel_id=1, replica_groups={{0,1,2,3},{4,5,6,7},{8,9,10,11},{12,13,14,15},{16,17,18,19},{20,21,22,2..., dimensions={0} | all-to-all | bytes 2097152 | tf_op jit(solution)/shard_map/all_to_all | solution.py:31
  92.5 0.9 reduce_sum.32
  (5 shorter events, 0.0 us)
Async XLA Ops:
  2.5 4.5 %copy-start = (bf16[1,1,256,256]{3,2,1,0:T(8,128)(2,1)S(1)}, bf16[1,1,256,256]{3,2,1,0:T(8,128)(2,1)}, u32[]{:S(2)}) copy-start(bf16[1,1,256,256]{3,2,1,0:T(8,128)(2,1)} %param.6) | copy-start | bytes 393220
  2.5 39.3 %copy-start.1 = (s32[16]{0:T(128)S(1)}, s32[16]{0:T(128)}, u32[]{:S(2)}) copy-start(s32[16]{0:T(128)} %constant.91.clone) | copy-start | bytes 196
  2.5 39.3 %all-to-all-start = ((bf16[4,1040,256]{2,1,0:T(8,128)(2,1)}), bf16[4,1040,256]{2,1,0:T(8,128)(2,1)S(1)}, u32[]{:S(2)}, u32[]{:S(2)}) async-start(bf16[4,1040,256]{2,1,0:T(8,128)(2,1)} %shard_map.55), calls=%async_computation | async-start | bytes 4259840 | tf_op jit(solution)/shard_map/all_to_all | solution.py:31
  41.8 16.2 %collective-permute-start.1 = (bf16[4,256,256]{2,1,0:T(8,128)(2,1)}, bf16[4,256,256]{2,1,0:T(8,128)(2,1)S(1)}, u32[]{:S(2)}, u32[]{:S(2)}) collective-permute-start(bf16[4,256,256]{2,1,0:T(8,128)(2,1)} %bitcast.5), channel_id=1, source_target_pairs={{0,68},{1,69},{2,70},{3,71},{4,72},{5,73},{6,74},{7,75},{8,76},{9,... | collective-permute-start | bytes 1572872 | tf_op jit(solution)/shard_map/ppermute | solution.py:25
  43.7 16.9 %collective-permute-start.2 = (bf16[4,256,256]{2,1,0:T(8,128)(2,1)}, bf16[4,256,256]{2,1,0:T(8,128)(2,1)S(1)}, u32[]{:S(2)}, u32[]{:S(2)}) collective-permute-start(bf16[4,256,256]{2,1,0:T(8,128)(2,1)} %bitcast.5), channel_id=1, source_target_pairs={{0,124},{1,125},{2,126},{3,127},{4,64},{5,65},{6,66},{7,67},{8,68}... | collective-permute-start | bytes 1572872 | tf_op jit(solution)/shard_map/ppermute | solution.py:25
  48.6 18.1 %collective-permute-start = (bf16[4,256,256]{2,1,0:T(8,128)(2,1)}, bf16[4,256,256]{2,1,0:T(8,128)(2,1)}, u32[]{:S(2)}, u32[]{:S(2)}) collective-permute-start(bf16[4,256,256]{2,1,0:T(8,128)(2,1)} %bitcast.5), channel_id=1, source_target_pairs={{0,64},{1,65},{2,66},{3,67},{4,68},{5,69},{6,70},{7,71},{8,72},{9,... | collective-permute-start | bytes 1572872 | tf_op jit(solution)/shard_map/ppermute | solution.py:25
  58.7 11.9 %collective-permute-start.3 = (bf16[2,256,256]{2,1,0:T(8,128)(2,1)}, bf16[2,256,256]{2,1,0:T(8,128)(2,1)S(1)}, u32[]{:S(2)}, u32[]{:S(2)}) collective-permute-start(bf16[2,256,256]{2,1,0:T(8,128)(2,1)} %slice.22), channel_id=1, source_target_pairs={{0,4},{1,5},{2,6},{3,7},{4,8},{5,9},{6,10},{7,11},{8,12},{9,13},{1... | collective-permute-start | bytes 786440 | tf_op jit(solution)/shard_map/ppermute | solution.py:25
  61.3 9.8 %collective-permute-start.4 = (bf16[2,256,256]{2,1,0:T(8,128)(2,1)}, bf16[2,256,256]{2,1,0:T(8,128)(2,1)}, u32[]{:S(2)}, u32[]{:S(2)}) collective-permute-start(bf16[2,256,256]{2,1,0:T(8,128)(2,1)} %slice.23), channel_id=1, source_target_pairs={{0,60},{1,61},{2,62},{3,63},{4,0},{5,1},{6,2},{7,3},{8,4},{9,5},{1... | collective-permute-start | bytes 786440 | tf_op jit(solution)/shard_map/ppermute | solution.py:25

commit v3 on v2

--- a/solution.py
+++ b/solution.py
@@ -12,7 +12,7 @@
 
 META = 16
 
-APART = (0,) * 4 + (-1,) * 4 + (1,) * 4 + (2,) * 4
+APART = (0,) * 4 + (1,) * 4 + (-1,) * 4 + (2,) * 4
 
 
 def moved(block, dz, flip=False):
@@ -20,8 +20,8 @@
     route = []
     for g in range(groups):
         for t in range(tiles):
-            to = (g ^ 1 if flip else g) * tiles + (t + dz * XS) % tiles
-            route.append((g * tiles + t, to))
+            to = (t + (-dz if g % 2 else dz) * XS) % tiles
+            route.append((g * tiles + t, (g ^ 1 if flip else g) * tiles + to))
     return lax.ppermute(block, ("irrep", "tile"), route)
 
 
@@ -137,8 +137,8 @@
     amps = along_x(packed)
     mine = every_fourth(integrals[0])
     mine, amps = lax.optimization_barrier((mine, amps))
-    near, up, down = moved(mine, 0, True), moved(mine, 1, True), moved(mine, -1, True)
-    upper, lower = moved(up[:2], 1), moved(down[2:], -1)
+    one, near, other = moved(mine, 1, True), moved(mine, 0, True), moved(mine, -1, True)
+    far = moved(one, -1)
 
     numbers = amps[:, flat : flat + 2 * fanout, :own].astype(jnp.int32)
     target = numbers[:, :fanout].reshape(XS * tasks)
@@ -147,7 +147,9 @@
     source = task // tasks
     code = (source * own + task % own) * 64 + source * RT + slot
     place = jnp.arange(depth, dtype=jnp.int32)
-    place_z = (my_z + jnp.array(APART, jnp.int32)) % SKIP + SKIP * (place % SKIP)
+    toward = 1 - 2 * (lax.axis_index("irrep") % 2)
+    apart = toward * jnp.array(APART, jnp.int32)
+    place_z = (my_z + apart) % SKIP + SKIP * (place % SKIP)
     hot = target[None, :] == (place_z * XS + my_x)[:, None]
     hot_bf16 = hot.astype(jnp.bfloat16)
     earlier = (task[:, None] < task[None, :]).astype(jnp.bfloat16)
@@ -160,10 +162,10 @@
     listed = listed.reshape(depth * 8)
 
     total = multiply(
-        0, listed, counts, amps, (near, up, down), (spare + 1, rows, columns), jnp.float32
+        0, listed, counts, amps, (near, one, other), (spare + 1, rows, columns), jnp.float32
     )
     partial = multiply(
-        12, listed, counts, amps, (total, upper, lower), (spare, rows, columns), jnp.bfloat16
+        12, listed, counts, amps, (total, far), (spare, rows, columns), jnp.bfloat16
     )
     back = along_x(partial).reshape(XS, RT, rows, columns)
     return jnp.sum(back.astype(jnp.float32), axis=0).astype(jnp.bfloat16)[None]

time: 94.1 us -> 87.2 us (0.927)
  starting transfers between devices: 20.2 us -> 16.8 us
  waiting for transfers between devices: 7.17 us -> 4.07 us
  local copies, waits for them, and re-layouts: 1.7 us -> 0.27 us
    ppermute x5 -> x4, starting transfers between devices: 15.7 us -> 12.4 us  [moved(): return lax.ppermute(block, ('irrep', 'tile'), route)]
    ppermute x5 -> x4, waiting for transfers between devices: 7.17 us -> 4.07 us  [moved(): return lax.ppermute(block, ('irrep', 'tile'), route)]
    slice x2 -> x0, local copies, waits for them, and re-layouts: 1.43 us -> none  [per_device(): upper, lower = (moved(up[:2], 1), moved(down[2:], -1))]
  transfers between devices with their start and end apart: 6 -> 5, of which waited for: 2 -> 3; matrix products, arithmetic and copies ran while one was open for 3% -> 1% of each run, Pallas kernels for 4% -> 5%
where the time goes in v3:
time: 87.2 us; the launch traced here: 86.8 us
  blocking collectives  54.8 us (63%)
  starting transfers between devices  16.8 us (19%)
  Pallas kernels  8.9 us (10%)
  waiting for transfers between devices  4.07 us (5%)
  other arithmetic  1.56 us (2%)
    all_gather x1, blocking collectives, every_fourth(): lax.all_gather(block, 'tile', axis=0, axis_index_groups=groups, tiled=True)  34.9 us
    all_to_all x1, blocking collectives, along_x(): lax.all_to_all(block, 'tile', split_axis=0, concat_axis=0, axis_index_gro...  19.9 us
    ppermute x4, starting transfers between devices, moved(): return lax.ppermute(block, ('irrep', 'tile'), route)  12.4 us
    pallas_call x2, Pallas kernels, multiply(): pl.pallas_call(functools.partial(ladder, first), out_shape=jax.ShapeDtype...  6.42 us
    all_to_all x1, starting transfers between devices, along_x(): lax.all_to_all(block, 'tile', split_axis=0, concat_axis=0, axis_index_gro...  4.44 us
    ppermute x4, waiting for transfers between devices, moved(): return lax.ppermute(block, ('irrep', 'tile'), route)  4.07 us
    pallas_call x1, Pallas kernels, per_device(): pl.pallas_call(pack, out_shape=jax.ShapeDtypeStruct((XS, flat + META, col...  2.48 us
  transfers between devices with their start and end apart: 5, of which 3 were waited for; matrix products, arithmetic and copies ran while one was open for 1% of the time, Pallas kernels for 5%

profile of v3, /device:TPU:24, one launch (start us, length us, event | category | flops | bytes accessed | tf_op | source)
XLA Modules:
  0.0 86.8 jit_solution(3730247828168683933)
XLA Ops:
  0.0 2.5 %shard_map.55 = bf16[4,1040,256]{2,1,0:T(8,128)(2,1)} custom-call(bf16[1024,256]{1,0:T(8,128)(2,1)} %bitcast.11, s32[2,16]{1,0:T(2,128)} %bitcast.12, s32[2,16]{1,0:T(2,128)} %bitcast.13), custom_call_target="tpu_custom_call" | custom-call | tf_op jit(solution)/shard_map/pallas_call | solution.py:126
  2.5 0.0 copy-start
  2.5 0.0 copy-start.1
  2.5 4.4 %all-to-all-start = ((bf16[4,1040,256]{2,1,0:T(8,128)(2,1)}), bf16[4,1040,256]{2,1,0:T(8,128)(2,1)S(1)}, u32[]{:S(2)}, u32[]{:S(2)}) async-start(bf16[4,1040,256]{2,1,0:T(8,128)(2,1)} %shard_map.55), calls=%async_computation | async-start | bytes 4259840 | tf_op jit(solution)/shard_map/all_to_all | solution.py:31
  6.9 0.0 copy-done
  7.0 34.9 %all-gather = bf16[4,1,256,256]{3,2,1,0:T(8,128)(2,1)} all-gather(bf16[1,1,256,256]{3,2,1,0:T(8,128)(2,1)S(1)} %copy-done), channel_id=2, replica_groups={{0,16,32,48},{1,17,33,49},{2,18,34,50},{3,19,35,51},{4,20,36,52},{5,21,..., dimensions={0}, use_global_device_ids=true | all-gather | bytes 655360 | tf_op jit(solution)/shard_map/all_gather | solution.py:40
  41.8 0.0 copy-done.1
  41.8 0.0 all-to-all-done.amps
  41.8 1.9 %collective-permute-start.1 = (bf16[4,256,256]{2,1,0:T(8,128)(2,1)}, bf16[4,256,256]{2,1,0:T(8,128)(2,1)S(1)}, u32[]{:S(2)}, u32[]{:S(2)}) collective-permute-start(bf16[4,256,256]{2,1,0:T(8,128)(2,1)} %bitcast.5), channel_id=1, source_target_pairs={{0,68},{1,69},{2,70},{3,71},{4,72},{5,73},{6,74},{7,75},{8,76},{9,... | collective-permute-start | bytes 1572872 | tf_op jit(solution)/shard_map/ppermute | solution.py:25
  43.8 3.3 %collective-permute-start = (bf16[4,256,256]{2,1,0:T(8,128)(2,1)}, bf16[4,256,256]{2,1,0:T(8,128)(2,1)S(1)}, u32[]{:S(2)}, u32[]{:S(2)}) collective-permute-start(bf16[4,256,256]{2,1,0:T(8,128)(2,1)} %bitcast.5), channel_id=1, source_target_pairs={{0,64},{1,65},{2,66},{3,67},{4,68},{5,69},{6,70},{7,71},{8,72},{9,... | collective-permute-start | bytes 1572872 | tf_op jit(solution)/shard_map/ppermute | solution.py:25
  47.1 2.5 %collective-permute-start.2 = (bf16[4,256,256]{2,1,0:T(8,128)(2,1)}, bf16[4,256,256]{2,1,0:T(8,128)(2,1)}, u32[]{:S(2)}, u32[]{:S(2)}) collective-permute-start(bf16[4,256,256]{2,1,0:T(8,128)(2,1)} %bitcast.5), channel_id=1, source_target_pairs={{0,124},{1,125},{2,126},{3,127},{4,64},{5,65},{6,66},{7,67},{8,68}... | collective-permute-start | bytes 1572872 | tf_op jit(solution)/shard_map/ppermute | solution.py:25
  49.6 0.1 eq.40
  49.7 0.1 reshape.41
  49.8 0.1 broadcast_compare_fusion
  49.9 0.2 convolution_convert_fusion
  50.1 2.6 %collective-permute-done.1.refs_1_ = bf16[4,256,256]{2,1,0:T(8,128)(2,1)S(1)} collective-permute-done((bf16[4,256,256]{2,1,0:T(8,128)(2,1)}, bf16[4,256,256]{2,1,0:T(8,128)(2,1)S(1)}, u32[]{:S(2)}, u32[]{:S(2)}) %collective-permute-start.1) | collective-permute-done | bytes 524320 | tf_op jit(solution)/shard_map/ppermute | solution.py:25
  52.7 4.7 %collective-permute-start.3 = (bf16[4,256,256]{2,1,0:T(8,128)(2,1)S(1)}, bf16[4,256,256]{2,1,0:T(8,128)(2,1)}, u32[]{:S(2)}, u32[]{:S(2)}) collective-permute-start(bf16[4,256,256]{2,1,0:T(8,128)(2,1)S(1)} %collective-permute-done.1.refs_1_), channel_id=1, source_target_pairs={{0,60},{1,61},{2,62},{3,63},{4,0},{5,1},{6,2},{7,3},{8,4},{9,5},{1... | collective-permute-start | bytes 1572872 | tf_op jit(solution)/shard_map/ppermute | solution.py:25
  57.4 0.3 select_reduce_fusion
  57.7 0.1 add.75.listed
  57.8 0.2 convert_reduce_fusion.counts
  58.0 0.0 collective-permute-done.refs_0_
  58.0 1.1 %collective-permute-done.2.refs_2_ = bf16[4,256,256]{2,1,0:T(8,128)(2,1)} collective-permute-done((bf16[4,256,256]{2,1,0:T(8,128)(2,1)}, bf16[4,256,256]{2,1,0:T(8,128)(2,1)}, u32[]{:S(2)}, u32[]{:S(2)}) %collective-permute-start.2) | collective-permute-done | bytes 524320 | tf_op jit(solution)/shard_map/ppermute | solution.py:25
  59.1 4.6 %shard_map.56.refs_0_ = f32[33,64,256]{2,1,0:T(8,128)S(1)} custom-call(s32[128]{0:T(128)S(1)} %add.75.listed, s32[16]{0:T(128)S(1)} %convert_reduce_fusion.counts, bf16[4,1040,256]{2,1,0:T(8,128)(2,1)S(1)} %all-to-all-done.amps, bf16[4,256,256]{2,1,0:T(8,128)(2,1)S(1)} %collective-permute-done.refs_0_, ...), custom_call_target="tpu_custom_call" | custom-call | flops 268435456 | bytes 8388608 | tf_op jit(solution)/shard_map/pallas_call | solution.py:102
  63.7 0.4 collective-permute-done.3.refs_1_
  64.0 1.9 %shard_map.57 = bf16[32,64,256]{2,1,0:T(8,128)(2,1)S(1)} custom-call(s32[128]{0:T(128)S(1)} %add.75.listed, s32[16]{0:T(128)S(1)} %convert_reduce_fusion.counts, bf16[4,1040,256]{2,1,0:T(8,128)(2,1)S(1)} %all-to-all-done.amps, f32[33,64,256]{2,1,0:T(8,128)S(1)} %shard_map.56.refs_0_, bf16[4,256,256]{2,1,0:T(8,128)(2,1)} %collective-permute-done.3.refs_1_), custom_call_target="tpu_custom_call" | custom-call | flops 268435456 | bytes 8388608 | tf_op jit(solution)/shard_map/pallas_call | solution.py:102
  65.9 19.9 %all_to_all.10 = bf16[32,64,256]{2,1,0:T(8,128)(2,1)S(1)} all-to-all(bf16[32,64,256]{2,1,0:T(8,128)(2,1)S(1)} %shard_map.57), channel_id=1, replica_groups={{0,1,2,3},{4,5,6,7},{8,9,10,11},{12,13,14,15},{16,17,18,19},{20,21,22,2..., dimensions={0} | all-to-all | bytes 2097152 | tf_op jit(solution)/shard_map/all_to_all | solution.py:31
  85.8 0.9 %reduce_sum.32 = bf16[8,64,256]{2,1,0:T(8,128)(2,1)} reduce(bf16[4,8,64,256]{3,2,1,0:T(8,128)(2,1)S(1)} %bitcast.10, bf16[]{:T(256)} %constant.104.clone.1), dimensions={0}, to_apply=%region_2.3 | reduce | flops 393216 | bytes 1310722 | tf_op jit(solution)/shard_map/reduce_sum | solution.py:171
  (5 shorter events, 0.0 us)
Async XLA Ops:
  2.5 4.5 %copy-start = (bf16[1,1,256,256]{3,2,1,0:T(8,128)(2,1)S(1)}, bf16[1,1,256,256]{3,2,1,0:T(8,128)(2,1)}, u32[]{:S(2)}) copy-start(bf16[1,1,256,256]{3,2,1,0:T(8,128)(2,1)} %param.6) | copy-start | bytes 393220
  2.5 39.3 %copy-start.1 = (s32[16]{0:T(128)S(1)}, s32[16]{0:T(128)}, u32[]{:S(2)}) copy-start(s32[16]{0:T(128)} %constant.105.clone) | copy-start | bytes 196
  2.5 39.3 %all-to-all-start = ((bf16[4,1040,256]{2,1,0:T(8,128)(2,1)}), bf16[4,1040,256]{2,1,0:T(8,128)(2,1)S(1)}, u32[]{:S(2)}, u32[]{:S(2)}) async-start(bf16[4,1040,256]{2,1,0:T(8,128)(2,1)} %shard_map.55), calls=%async_computation | async-start | bytes 4259840 | tf_op jit(solution)/shard_map/all_to_all | solution.py:31
  41.8 10.8 %collective-permute-start.1 = (bf16[4,256,256]{2,1,0:T(8,128)(2,1)}, bf16[4,256,256]{2,1,0:T(8,128)(2,1)S(1)}, u32[]{:S(2)}, u32[]{:S(2)}) collective-permute-start(bf16[4,256,256]{2,1,0:T(8,128)(2,1)} %bitcast.5), channel_id=1, source_target_pairs={{0,68},{1,69},{2,70},{3,71},{4,72},{5,73},{6,74},{7,75},{8,76},{9,... | collective-permute-start | bytes 1572872 | tf_op jit(solution)/shard_map/ppermute | solution.py:25
  43.8 14.2 %collective-permute-start = (bf16[4,256,256]{2,1,0:T(8,128)(2,1)}, bf16[4,256,256]{2,1,0:T(8,128)(2,1)S(1)}, u32[]{:S(2)}, u32[]{:S(2)}) collective-permute-start(bf16[4,256,256]{2,1,0:T(8,128)(2,1)} %bitcast.5), channel_id=1, source_target_pairs={{0,64},{1,65},{2,66},{3,67},{4,68},{5,69},{6,70},{7,71},{8,72},{9,... | collective-permute-start | bytes 1572872 | tf_op jit(solution)/shard_map/ppermute | solution.py:25
  47.1 12.0 %collective-permute-start.2 = (bf16[4,256,256]{2,1,0:T(8,128)(2,1)}, bf16[4,256,256]{2,1,0:T(8,128)(2,1)}, u32[]{:S(2)}, u32[]{:S(2)}) collective-permute-start(bf16[4,256,256]{2,1,0:T(8,128)(2,1)} %bitcast.5), channel_id=1, source_target_pairs={{0,124},{1,125},{2,126},{3,127},{4,64},{5,65},{6,66},{7,67},{8,68}... | collective-permute-start | bytes 1572872 | tf_op jit(solution)/shard_map/ppermute | solution.py:25
  52.7 11.3 %collective-permute-start.3 = (bf16[4,256,256]{2,1,0:T(8,128)(2,1)S(1)}, bf16[4,256,256]{2,1,0:T(8,128)(2,1)}, u32[]{:S(2)}, u32[]{:S(2)}) collective-permute-start(bf16[4,256,256]{2,1,0:T(8,128)(2,1)S(1)} %collective-permute-done.1.refs_1_), channel_id=1, source_target_pairs={{0,60},{1,61},{2,62},{3,63},{4,0},{5,1},{6,2},{7,3},{8,4},{9,5},{1... | collective-permute-start | bytes 1572872 | tf_op jit(solution)/shard_map/ppermute | solution.py:25

commit v4 on v3

v4 whole, which is shorter than its diff:
```python
import functools
import jax
import jax.numpy as jnp
from jax import lax
from jax.experimental import pallas as pl
from jax.experimental.pallas import tpu as pltpu
from jax.sharding import PartitionSpec as P

RT = 8
XS = 4
SKIP = 4

META = 16

APART = (0,) * 4 + (1,) * 4 + (-1,) * 4 + (2,) * 4


def moved(block, dz, flip=False):
    groups, tiles = lax.axis_size("irrep"), lax.axis_size("tile")
    route = []
    for g in range(groups):
        for t in range(tiles):
            to = (t + (-dz if g % 2 else dz) * XS) % tiles
            route.append((g * tiles + t, (g ^ 1 if flip else g) * tiles + to))
    return lax.ppermute(block, ("irrep", "tile"), route)


def along_x(block):
    tiles = lax.axis_size("tile")
    rows = [list(range(low, low + XS)) for low in range(0, tiles, XS)]
    return lax.all_to_all(
        block, "tile", split_axis=0, concat_axis=0, axis_index_groups=rows, tiled=True
    )


def every_fourth(block):
    tiles = lax.axis_size("tile")
    step = SKIP * XS
    groups = [list(range(low, tiles, step)) for low in range(step)]
    return lax.all_gather(block, "tile", axis=0, axis_index_groups=groups, tiled=True)


def pack(amps, targets, slots, out, held, numbers, meta, sems):
    size, (fanout, count) = amps.shape[0], targets.shape
    part = size // XS
    pieces = [pl.ds(i * part, part) for i in range(XS)]
    reads = [
        pltpu.make_async_copy(amps.at[piece], held.at[piece], sems.at[XS, i])
        for i, piece in enumerate(pieces)
    ]
    reads += [
        pltpu.make_async_copy(ref, numbers.at[i], sems.at[XS + 1, i])
        for i, ref in enumerate((targets, slots))
    ]
    for copy in reads:
        copy.start()
    writes = []
    for i, piece in enumerate(pieces):
        reads[i].wait()
        for x in range(XS):
            writes.append(
                pltpu.make_async_copy(held.at[piece], out.at[x, piece], sems.at[x, i])
            )
            writes[-1].start()
    for copy in reads[XS:]:
        copy.wait()
    rows = jnp.concatenate([numbers[0], numbers[1]], axis=0).astype(jnp.float32)
    rows = jnp.pad(rows, ((0, META - 2 * fanout), (0, out.shape[2] - count)))
    meta[...] = rows.astype(meta.dtype)
    for x in range(XS):
        writes.append(
            pltpu.make_async_copy(meta, out.at[x, pl.ds(size, META)], sems.at[x, XS])
        )
        writes[-1].start()
    for copy in writes:
        copy.wait()


def add_products(first, listed, counts, amps, held, total):
    rows = total.shape[1]
    own = (amps.shape[1] - META) // rows
    tiles = [(ref, k) for ref in held for k in range(ref.shape[0])]

    def pair(place, q):
        codes = [listed[place * 8 + 2 * q + i] for i in range(2)]
        parts = []
        for code in codes:
            index = code >> 6
            start = pl.multiple_of((index % own) * rows, rows)
            parts.append(amps[index // own, pl.ds(start, rows), :])
        ref, k = tiles[place - first]
        tasks = jnp.concatenate(parts, axis=0)
        return codes, jnp.dot(tasks, ref[k], preferred_element_type=jnp.float32)

    def add(codes, product):
        for i, code in enumerate(codes):
            total[code & 63] += product[i * rows : (i + 1) * rows]

    for low in range(first, first + len(tiles), 4):
        for codes, product in [pair(place, 0) for place in range(low, low + 4)]:
            add(codes, product)
    for place in range(first, first + len(tiles)):

        def more(q, carry, place=place):
            add(*pair(place, q))
            return carry

        lax.fori_loop(1, (counts[place] + 1) // 2, more, 0)


def early(listed, counts, amps, *refs):
    held, total = refs[:-1], refs[-1]
    total[...] = jnp.zeros_like(total)
    add_products(0, listed, counts, amps, held, total)


def late(first, listed, counts, amps, before, held, out, total):
    total[...] = before[...]
    add_products(first, listed, counts, amps, (held,), total)
    out[...] = total[: out.shape[0]].astype(out.dtype)


def per_device(amplitudes, integrals, executors, residual_slots):
    own, rows, columns = amplitudes.shape[1:]
    fanout = executors.shape[2]
    tasks = own * fanout
    depth = lax.axis_size("tile") // XS
    me = lax.axis_index("tile")
    my_x, my_z = me % XS, me // XS

    vmem = pl.BlockSpec(memory_space=pltpu.VMEM)
    smem = pl.BlockSpec(memory_space=pltpu.SMEM)
    anywhere = pl.BlockSpec(memory_space=pl.ANY)
    flat = own * rows
    packed = pl.pallas_call(
        pack,
        out_shape=jax.ShapeDtypeStruct((XS, flat + META, columns), jnp.bfloat16),
        in_specs=[anywhere] * 3,
        out_specs=anywhere,
        scratch_shapes=[
            pltpu.VMEM((flat, columns), jnp.bfloat16),
            pltpu.VMEM((2, fanout, own), jnp.int32),
            pltpu.VMEM((META, columns), jnp.bfloat16),
            pltpu.SemaphoreType.DMA((XS + 2, XS + 1)),
        ],
    )(amplitudes.reshape(flat, columns), executors[0].T, residual_slots[0].T)
    integrals, packed = lax.optimization_barrier((integrals, packed))
    amps = along_x(packed)
    mine = every_fourth(integrals[0])
    mine, amps = lax.optimization_barrier((mine, amps))
    one, near, other = moved(mine, 1, True), moved(mine, 0, True), moved(mine, -1, True)
    far = moved(one, -1)

    numbers = amps[:, flat : flat + 2 * fanout, :own].astype(jnp.int32)
    target = numbers[:, :fanout].reshape(XS * tasks)
    slot = numbers[:, fanout:].reshape(XS * tasks)
    task = jnp.arange(XS * tasks, dtype=jnp.int32)
    source = task // tasks
    code = (source * own + task % own) * 64 + source * RT + slot
    place = jnp.arange(depth, dtype=jnp.int32)
    toward = 1 - 2 * (lax.axis_index("irrep") % 2)
    apart = toward * jnp.array(APART, jnp.int32)
    place_z = (my_z + apart) % SKIP + SKIP * (place % SKIP)
    hot = target[None, :] == (place_z * XS + my_x)[:, None]
    hot_bf16 = hot.astype(jnp.bfloat16)
    earlier = (task[:, None] < task[None, :]).astype(jnp.bfloat16)
    rank = jnp.dot(hot_bf16, earlier, preferred_element_type=jnp.float32).astype(jnp.int32)
    counts = jnp.sum(hot.astype(jnp.int32), axis=1)
    ranks = jnp.arange(8, dtype=jnp.int32)
    chosen = hot[:, None, :] & (rank[:, None, :] == ranks[None, :, None])
    spare = XS * RT
    listed = spare + jnp.sum(jnp.where(chosen, code - spare, 0), axis=2)
    listed = listed.reshape(depth * 8)

    total_shape = (spare + 1, rows, columns)
    params = pltpu.CompilerParams(vmem_limit_bytes=12 * 1024 * 1024)
    total = pl.pallas_call(
        early,
        out_shape=jax.ShapeDtypeStruct(total_shape, jnp.float32),
        in_specs=[smem] * 2 + [vmem] * 4,
        out_specs=vmem,
        compiler_params=params,
        cost_estimate=pl.CostEstimate(flops=1 << 28, bytes_accessed=1 << 23, transcendentals=0),
    )(listed, counts, amps, near, one, other)
    partial = pl.pallas_call(
        functools.partial(late, 12),
        out_shape=jax.ShapeDtypeStruct((spare, rows, columns), jnp.bfloat16),
        in_specs=[smem] * 2 + [vmem] * 3,
        out_specs=vmem,
        scratch_shapes=[pltpu.VMEM(total_shape, jnp.float32)],
        compiler_params=params,
        cost_estimate=pl.CostEstimate(flops=1 << 28, bytes_accessed=1 << 23, transcendentals=0),
    )(listed, counts, amps, total, far)
    back = along_x(partial).reshape(XS, RT, rows, columns)
    return jnp.sum(back.astype(jnp.float32), axis=0).astype(jnp.bfloat16)[None]


def solution(mesh):
    placed = (
        P("irrep", "tile", None, None),
        P("irrep", "tile", None, None),
        P("irrep", "tile", None),
        P("irrep", "tile", None),
    )
    return jax.shard_map(
        per_device,
        mesh=mesh,
        in_specs=placed,
        out_specs=P("irrep", "tile", None, None),
        check_vma=False,
    )
```

time: 87.2 us -> 87.2 us (level)
  Pallas kernels: 8.9 us -> 6.88 us
  waiting for transfers between devices: 4.07 us -> 5.72 us
    pallas_call x2, Pallas kernels: 6.42 us -> 4.38 us  [the longest x1 2.9 us: per_device(): pl.pallas_call(early, out_shape=jax.ShapeDtypeStruct(total_shape, jnp.flo...]
    ppermute x4, waiting for transfers between devices: 4.07 us -> 5.72 us  [moved(): return lax.ppermute(block, ('irrep', 'tile'), route)]
  transfers between devices with their start and end apart: 5 -> 5, of which waited for: 3 -> 3; matrix products, arithmetic and copies ran while one was open for 1% -> 1% of each run, Pallas kernels for 5% -> 3%
where the time goes in v4:
time: 87.2 us; the launch traced here: 86.6 us
  blocking collectives  55 us (63%)
  starting transfers between devices  16.8 us (19%)
  Pallas kernels  6.88 us (8%)
  waiting for transfers between devices  5.72 us (7%)
  other arithmetic  1.56 us (2%)
    all_gather x1, blocking collectives, every_fourth(): lax.all_gather(block, 'tile', axis=0, axis_index_groups=groups, tiled=True)  34.9 us
    all_to_all x1, blocking collectives, along_x(): lax.all_to_all(block, 'tile', split_axis=0, concat_axis=0, axis_index_gro...  20.2 us
    ppermute x4, starting transfers between devices, moved(): return lax.ppermute(block, ('irrep', 'tile'), route)  12.4 us
    ppermute x4, waiting for transfers between devices, moved(): return lax.ppermute(block, ('irrep', 'tile'), route)  5.72 us
    all_to_all x1, starting transfers between devices, along_x(): lax.all_to_all(block, 'tile', split_axis=0, concat_axis=0, axis_index_gro...  4.44 us
    pallas_call x1, Pallas kernels, per_device(): pl.pallas_call(early, out_shape=jax.ShapeDtypeStruct(total_shape, jnp.flo...  2.9 us
    pallas_call x1, Pallas kernels, per_device(): pl.pallas_call(pack, out_shape=jax.ShapeDtypeStruct((XS, flat + META, col...  2.5 us
  transfers between devices with their start and end apart: 5, of which 3 were waited for; matrix products, arithmetic and copies ran while one was open for 1% of the time, Pallas kernels for 3%

profile of v4, /device:TPU:24, one launch (start us, length us, event | category | flops | bytes accessed | tf_op | source)
XLA Modules:
  0.0 86.6 jit_solution(7493780862346412198)
XLA Ops:
  0.0 2.5 %shard_map.55 = bf16[4,1040,256]{2,1,0:T(8,128)(2,1)} custom-call(bf16[1024,256]{1,0:T(8,128)(2,1)} %bitcast.11, s32[2,16]{1,0:T(2,128)} %bitcast.12, s32[2,16]{1,0:T(2,128)} %bitcast.13), custom_call_target="tpu_custom_call" | custom-call | tf_op jit(solution)/shard_map/pallas_call | solution.py:135
  2.5 0.0 copy-start
  2.5 0.0 copy-start.1
  2.5 4.4 %all-to-all-start = ((bf16[4,1040,256]{2,1,0:T(8,128)(2,1)}), bf16[4,1040,256]{2,1,0:T(8,128)(2,1)S(1)}, u32[]{:S(2)}, u32[]{:S(2)}) async-start(bf16[4,1040,256]{2,1,0:T(8,128)(2,1)} %shard_map.55), calls=%async_computation | async-start | bytes 4259840 | tf_op jit(solution)/shard_map/all_to_all | solution.py:31
  7.0 0.0 copy-done
  7.0 34.9 %all-gather = bf16[4,1,256,256]{3,2,1,0:T(8,128)(2,1)} all-gather(bf16[1,1,256,256]{3,2,1,0:T(8,128)(2,1)S(1)} %copy-done), channel_id=2, replica_groups={{0,16,32,48},{1,17,33,49},{2,18,34,50},{3,19,35,51},{4,20,36,52},{5,21,..., dimensions={0}, use_global_device_ids=true | all-gather | bytes 655360 | tf_op jit(solution)/shard_map/all_gather | solution.py:40
  41.8 0.0 copy-done.1
  41.8 0.0 all-to-all-done.amps
  41.9 1.9 %collective-permute-start.1 = (bf16[4,256,256]{2,1,0:T(8,128)(2,1)}, bf16[4,256,256]{2,1,0:T(8,128)(2,1)S(1)}, u32[]{:S(2)}, u32[]{:S(2)}) collective-permute-start(bf16[4,256,256]{2,1,0:T(8,128)(2,1)} %bitcast.5), channel_id=1, source_target_pairs={{0,68},{1,69},{2,70},{3,71},{4,72},{5,73},{6,74},{7,75},{8,76},{9,... | collective-permute-start | bytes 1572872 | tf_op jit(solution)/shard_map/ppermute | solution.py:25
  43.8 3.3 %collective-permute-start = (bf16[4,256,256]{2,1,0:T(8,128)(2,1)}, bf16[4,256,256]{2,1,0:T(8,128)(2,1)S(1)}, u32[]{:S(2)}, u32[]{:S(2)}) collective-permute-start(bf16[4,256,256]{2,1,0:T(8,128)(2,1)} %bitcast.5), channel_id=1, source_target_pairs={{0,64},{1,65},{2,66},{3,67},{4,68},{5,69},{6,70},{7,71},{8,72},{9,... | collective-permute-start | bytes 1572872 | tf_op jit(solution)/shard_map/ppermute | solution.py:25
  47.1 2.5 %collective-permute-start.2 = (bf16[4,256,256]{2,1,0:T(8,128)(2,1)}, bf16[4,256,256]{2,1,0:T(8,128)(2,1)}, u32[]{:S(2)}, u32[]{:S(2)}) collective-permute-start(bf16[4,256,256]{2,1,0:T(8,128)(2,1)} %bitcast.5), channel_id=1, source_target_pairs={{0,124},{1,125},{2,126},{3,127},{4,64},{5,65},{6,66},{7,67},{8,68}... | collective-permute-start | bytes 1572872 | tf_op jit(solution)/shard_map/ppermute | solution.py:25
  49.7 0.1 eq.40
  49.7 0.1 reshape.41
  49.8 0.1 broadcast_compare_fusion
  49.9 0.2 convolution_convert_fusion
  50.1 2.6 %collective-permute-done.1.refs_1_ = bf16[4,256,256]{2,1,0:T(8,128)(2,1)S(1)} collective-permute-done((bf16[4,256,256]{2,1,0:T(8,128)(2,1)}, bf16[4,256,256]{2,1,0:T(8,128)(2,1)S(1)}, u32[]{:S(2)}, u32[]{:S(2)}) %collective-permute-start.1) | collective-permute-done | bytes 524320 | tf_op jit(solution)/shard_map/ppermute | solution.py:25
  52.7 4.7 %collective-permute-start.3 = (bf16[4,256,256]{2,1,0:T(8,128)(2,1)S(1)}, bf16[4,256,256]{2,1,0:T(8,128)(2,1)}, u32[]{:S(2)}, u32[]{:S(2)}) collective-permute-start(bf16[4,256,256]{2,1,0:T(8,128)(2,1)S(1)} %collective-permute-done.1.refs_1_), channel_id=1, source_target_pairs={{0,60},{1,61},{2,62},{3,63},{4,0},{5,1},{6,2},{7,3},{8,4},{9,5},{1... | collective-permute-start | bytes 1572872 | tf_op jit(solution)/shard_map/ppermute | solution.py:25
  57.4 0.3 select_reduce_fusion
  57.7 0.1 add.75.listed
  57.8 0.2 convert_reduce_fusion.counts
  58.0 0.0 collective-permute-done.refs_0_
  58.0 1.1 %collective-permute-done.2.refs_2_ = bf16[4,256,256]{2,1,0:T(8,128)(2,1)} collective-permute-done((bf16[4,256,256]{2,1,0:T(8,128)(2,1)}, bf16[4,256,256]{2,1,0:T(8,128)(2,1)}, u32[]{:S(2)}, u32[]{:S(2)}) %collective-permute-start.2) | collective-permute-done | bytes 524320 | tf_op jit(solution)/shard_map/ppermute | solution.py:25
  59.1 2.9 %shard_map.56.before = f32[33,64,256]{2,1,0:T(8,128)S(1)} custom-call(s32[128]{0:T(128)S(1)} %add.75.listed, s32[16]{0:T(128)S(1)} %convert_reduce_fusion.counts, bf16[4,1040,256]{2,1,0:T(8,128)(2,1)S(1)} %all-to-all-done.amps, bf16[4,256,256]{2,1,0:T(8,128)(2,1)S(1)} %collective-permute-done.refs_0_, ...), custom_call_target="tpu_custom_call" | custom-call | flops 268435456 | bytes 8388608 | tf_op jit(solution)/shard_map/pallas_call | solution.py:177
  62.0 2.0 %collective-permute-done.3.held = bf16[4,256,256]{2,1,0:T(8,128)(2,1)} collective-permute-done((bf16[4,256,256]{2,1,0:T(8,128)(2,1)S(1)}, bf16[4,256,256]{2,1,0:T(8,128)(2,1)}, u32[]{:S(2)}, u32[]{:S(2)}) %collective-permute-start.3) | collective-permute-done | bytes 524320 | tf_op jit(solution)/shard_map/ppermute | solution.py:25
  64.0 1.5 %shard_map.57 = bf16[32,64,256]{2,1,0:T(8,128)(2,1)S(1)} custom-call(s32[128]{0:T(128)S(1)} %add.75.listed, s32[16]{0:T(128)S(1)} %convert_reduce_fusion.counts, bf16[4,1040,256]{2,1,0:T(8,128)(2,1)S(1)} %all-to-all-done.amps, f32[33,64,256]{2,1,0:T(8,128)S(1)} %shard_map.56.before, bf16[4,256,256]{2,1,0:T(8,128)(2,1)} %collective-permute-done.3.held), custom_call_target="tpu_custom_call" | custom-call | flops 268435456 | bytes 8388608 | tf_op jit(solution)/shard_map/pallas_call | solution.py:185
  65.5 20.2 %all_to_all.10 = bf16[32,64,256]{2,1,0:T(8,128)(2,1)S(1)} all-to-all(bf16[32,64,256]{2,1,0:T(8,128)(2,1)S(1)} %shard_map.57), channel_id=1, replica_groups={{0,1,2,3},{4,5,6,7},{8,9,10,11},{12,13,14,15},{16,17,18,19},{20,21,22,2..., dimensions={0} | all-to-all | bytes 2097152 | tf_op jit(solution)/shard_map/all_to_all | solution.py:31
  85.7 0.9 %reduce_sum.32 = bf16[8,64,256]{2,1,0:T(8,128)(2,1)} reduce(bf16[4,8,64,256]{3,2,1,0:T(8,128)(2,1)S(1)} %bitcast.10, bf16[]{:T(256)} %constant.104.clone.1), dimensions={0}, to_apply=%region_2.3 | reduce | flops 393216 | bytes 1310722 | tf_op jit(solution)/shard_map/reduce_sum | solution.py:195
  (5 shorter events, 0.0 us)
Async XLA Ops:
  2.5 4.5 %copy-start = (bf16[1,1,256,256]{3,2,1,0:T(8,128)(2,1)S(1)}, bf16[1,1,256,256]{3,2,1,0:T(8,128)(2,1)}, u32[]{:S(2)}) copy-start(bf16[1,1,256,256]{3,2,1,0:T(8,128)(2,1)} %param.6) | copy-start | bytes 393220
  2.5 39.3 %copy-start.1 = (s32[16]{0:T(128)S(1)}, s32[16]{0:T(128)}, u32[]{:S(2)}) copy-start(s32[16]{0:T(128)} %constant.105.clone) | copy-start | bytes 196
  2.5 39.3 %all-to-all-start = ((bf16[4,1040,256]{2,1,0:T(8,128)(2,1)}), bf16[4,1040,256]{2,1,0:T(8,128)(2,1)S(1)}, u32[]{:S(2)}, u32[]{:S(2)}) async-start(bf16[4,1040,256]{2,1,0:T(8,128)(2,1)} %shard_map.55), calls=%async_computation | async-start | bytes 4259840 | tf_op jit(solution)/shard_map/all_to_all | solution.py:31
  41.9 10.8 %collective-permute-start.1 = (bf16[4,256,256]{2,1,0:T(8,128)(2,1)}, bf16[4,256,256]{2,1,0:T(8,128)(2,1)S(1)}, u32[]{:S(2)}, u32[]{:S(2)}) collective-permute-start(bf16[4,256,256]{2,1,0:T(8,128)(2,1)} %bitcast.5), channel_id=1, source_target_pairs={{0,68},{1,69},{2,70},{3,71},{4,72},{5,73},{6,74},{7,75},{8,76},{9,... | collective-permute-start | bytes 1572872 | tf_op jit(solution)/shard_map/ppermute | solution.py:25
  43.8 14.2 %collective-permute-start = (bf16[4,256,256]{2,1,0:T(8,128)(2,1)}, bf16[4,256,256]{2,1,0:T(8,128)(2,1)S(1)}, u32[]{:S(2)}, u32[]{:S(2)}) collective-permute-start(bf16[4,256,256]{2,1,0:T(8,128)(2,1)} %bitcast.5), channel_id=1, source_target_pairs={{0,64},{1,65},{2,66},{3,67},{4,68},{5,69},{6,70},{7,71},{8,72},{9,... | collective-permute-start | bytes 1572872 | tf_op jit(solution)/shard_map/ppermute | solution.py:25
  47.1 12.0 %collective-permute-start.2 = (bf16[4,256,256]{2,1,0:T(8,128)(2,1)}, bf16[4,256,256]{2,1,0:T(8,128)(2,1)}, u32[]{:S(2)}, u32[]{:S(2)}) collective-permute-start(bf16[4,256,256]{2,1,0:T(8,128)(2,1)} %bitcast.5), channel_id=1, source_target_pairs={{0,124},{1,125},{2,126},{3,127},{4,64},{5,65},{6,66},{7,67},{8,68}... | collective-permute-start | bytes 1572872 | tf_op jit(solution)/shard_map/ppermute | solution.py:25
  52.7 11.3 %collective-permute-start.3 = (bf16[4,256,256]{2,1,0:T(8,128)(2,1)S(1)}, bf16[4,256,256]{2,1,0:T(8,128)(2,1)}, u32[]{:S(2)}, u32[]{:S(2)}) collective-permute-start(bf16[4,256,256]{2,1,0:T(8,128)(2,1)S(1)} %collective-permute-done.1.refs_1_), channel_id=1, source_target_pairs={{0,60},{1,61},{2,62},{3,63},{4,0},{5,1},{6,2},{7,3},{8,4},{9,5},{1... | collective-permute-start | bytes 1572872 | tf_op jit(solution)/shard_map/ppermute | solution.py:25

commit v5 on v4

--- a/solution.py
+++ b/solution.py
@@ -20,7 +20,7 @@
     route = []
     for g in range(groups):
         for t in range(tiles):
-            to = (t + (-dz if g % 2 else dz) * XS) % tiles
+            to = (t + (dz if g % 2 else -dz) * XS) % tiles
             route.append((g * tiles + t, (g ^ 1 if flip else g) * tiles + to))
     return lax.ppermute(block, ("irrep", "tile"), route)
 
@@ -158,7 +158,7 @@
     source = task // tasks
     code = (source * own + task % own) * 64 + source * RT + slot
     place = jnp.arange(depth, dtype=jnp.int32)
-    toward = 1 - 2 * (lax.axis_index("irrep") % 2)
+    toward = 2 * (lax.axis_index("irrep") % 2) - 1
     apart = toward * jnp.array(APART, jnp.int32)
     place_z = (my_z + apart) % SKIP + SKIP * (place % SKIP)
     hot = target[None, :] == (place_z * XS + my_x)[:, None]

time: 87.2 us -> 85.6 us (0.982)
  waiting for transfers between devices: 5.72 us -> 12.7 us
  blocking collectives: 55 us -> 49.5 us
  starting transfers between devices: 16.8 us -> 12.9 us
    ppermute x4, waiting for transfers between devices: 5.72 us -> 12.7 us  [moved(): return lax.ppermute(block, ('irrep', 'tile'), route)]
    all_to_all x1, blocking collectives: 20.2 us -> 14.6 us  [along_x(): lax.all_to_all(block, 'tile', split_axis=0, concat_axis=0, axis_index_gro...]
    ppermute x4, starting transfers between devices: 12.4 us -> 8.5 us  [moved(): return lax.ppermute(block, ('irrep', 'tile'), route)]
  transfers between devices with their start and end apart: 5 -> 5, of which waited for: 3 -> 2; matrix products, arithmetic and copies ran while one was open for 1% -> 1% of each run, Pallas kernels for 3% -> 3%
where the time goes in v5:
time: 85.6 us; the launch traced here: 84.4 us
  blocking collectives  49.5 us (58%)
  starting transfers between devices  12.9 us (15%)
  waiting for transfers between devices  12.7 us (15%)
  Pallas kernels  7.09 us (8%)
  other arithmetic  1.56 us (2%)
    all_gather x1, blocking collectives, every_fourth(): lax.all_gather(block, 'tile', axis=0, axis_index_groups=groups, tiled=True)  34.9 us
    all_to_all x1, blocking collectives, along_x(): lax.all_to_all(block, 'tile', split_axis=0, concat_axis=0, axis_index_gro...  14.6 us
    ppermute x4, waiting for transfers between devices, moved(): return lax.ppermute(block, ('irrep', 'tile'), route)  12.7 us
    ppermute x4, starting transfers between devices, moved(): return lax.ppermute(block, ('irrep', 'tile'), route)  8.5 us
    all_to_all x1, starting transfers between devices, along_x(): lax.all_to_all(block, 'tile', split_axis=0, concat_axis=0, axis_index_gro...  4.44 us
    pallas_call x1, Pallas kernels, per_device(): pl.pallas_call(early, out_shape=jax.ShapeDtypeStruct(total_shape, jnp.flo...  2.94 us
    pallas_call x1, Pallas kernels, per_device(): pl.pallas_call(pack, out_shape=jax.ShapeDtypeStruct((XS, flat + META, col...  2.5 us
  transfers between devices with their start and end apart: 5, of which 2 were waited for; matrix products, arithmetic and copies ran while one was open for 1% of the time, Pallas kernels for 3%

profile of v5, /device:TPU:24, one launch (start us, length us, event | category | flops | bytes accessed | tf_op | source)
XLA Modules:
  0.0 84.4 jit_solution(3430281842449356289)
XLA Ops:
  0.0 2.5 %shard_map.55 = bf16[4,1040,256]{2,1,0:T(8,128)(2,1)} custom-call(bf16[1024,256]{1,0:T(8,128)(2,1)} %bitcast.11, s32[2,16]{1,0:T(2,128)} %bitcast.12, s32[2,16]{1,0:T(2,128)} %bitcast.13), custom_call_target="tpu_custom_call" | custom-call | tf_op jit(solution)/shard_map/pallas_call | solution.py:135
  2.5 0.0 copy-start
  2.5 0.0 copy-start.1
  2.5 4.4 %all-to-all-start = ((bf16[4,1040,256]{2,1,0:T(8,128)(2,1)}), bf16[4,1040,256]{2,1,0:T(8,128)(2,1)S(1)}, u32[]{:S(2)}, u32[]{:S(2)}) async-start(bf16[4,1040,256]{2,1,0:T(8,128)(2,1)} %shard_map.55), calls=%async_computation | async-start | bytes 4259840 | tf_op jit(solution)/shard_map/all_to_all | solution.py:31
  7.0 0.0 copy-done
  7.0 34.9 %all-gather = bf16[4,1,256,256]{3,2,1,0:T(8,128)(2,1)} all-gather(bf16[1,1,256,256]{3,2,1,0:T(8,128)(2,1)S(1)} %copy-done), channel_id=2, replica_groups={{0,16,32,48},{1,17,33,49},{2,18,34,50},{3,19,35,51},{4,20,36,52},{5,21,..., dimensions={0}, use_global_device_ids=true | all-gather | bytes 655360 | tf_op jit(solution)/shard_map/all_gather | solution.py:40
  41.8 0.0 copy-done.1
  41.8 0.0 all-to-all-done.amps
  41.9 1.9 %collective-permute-start.1 = (bf16[4,256,256]{2,1,0:T(8,128)(2,1)}, bf16[4,256,256]{2,1,0:T(8,128)(2,1)S(1)}, u32[]{:S(2)}, u32[]{:S(2)}) collective-permute-start(bf16[4,256,256]{2,1,0:T(8,128)(2,1)} %bitcast.5), channel_id=1, source_target_pairs={{0,124},{1,125},{2,126},{3,127},{4,64},{5,65},{6,66},{7,67},{8,68}... | collective-permute-start | bytes 1572872 | tf_op jit(solution)/shard_map/ppermute | solution.py:25
  43.8 1.9 %collective-permute-start = (bf16[4,256,256]{2,1,0:T(8,128)(2,1)}, bf16[4,256,256]{2,1,0:T(8,128)(2,1)S(1)}, u32[]{:S(2)}, u32[]{:S(2)}) collective-permute-start(bf16[4,256,256]{2,1,0:T(8,128)(2,1)} %bitcast.5), channel_id=1, source_target_pairs={{0,64},{1,65},{2,66},{3,67},{4,68},{5,69},{6,70},{7,71},{8,72},{9,... | collective-permute-start | bytes 1572872 | tf_op jit(solution)/shard_map/ppermute | solution.py:25
  45.7 2.8 %collective-permute-start.2 = (bf16[4,256,256]{2,1,0:T(8,128)(2,1)}, bf16[4,256,256]{2,1,0:T(8,128)(2,1)}, u32[]{:S(2)}, u32[]{:S(2)}) collective-permute-start(bf16[4,256,256]{2,1,0:T(8,128)(2,1)} %bitcast.5), channel_id=1, source_target_pairs={{0,68},{1,69},{2,70},{3,71},{4,72},{5,73},{6,74},{7,75},{8,76},{9,... | collective-permute-start | bytes 1572872 | tf_op jit(solution)/shard_map/ppermute | solution.py:25
  48.5 0.1 eq.40
  48.6 0.1 reshape.41
  48.7 0.1 broadcast_compare_fusion
  48.7 0.2 convolution_convert_fusion
  48.9 5.9 %collective-permute-done.1.refs_1_ = bf16[4,256,256]{2,1,0:T(8,128)(2,1)S(1)} collective-permute-done((bf16[4,256,256]{2,1,0:T(8,128)(2,1)}, bf16[4,256,256]{2,1,0:T(8,128)(2,1)S(1)}, u32[]{:S(2)}, u32[]{:S(2)}) %collective-permute-start.1) | collective-permute-done | bytes 524320 | tf_op jit(solution)/shard_map/ppermute | solution.py:25
  54.8 1.9 %collective-permute-start.3 = (bf16[4,256,256]{2,1,0:T(8,128)(2,1)S(1)}, bf16[4,256,256]{2,1,0:T(8,128)(2,1)}, u32[]{:S(2)}, u32[]{:S(2)}) collective-permute-start(bf16[4,256,256]{2,1,0:T(8,128)(2,1)S(1)} %collective-permute-done.1.refs_1_), channel_id=1, source_target_pairs={{0,4},{1,5},{2,6},{3,7},{4,8},{5,9},{6,10},{7,11},{8,12},{9,13},{1... | collective-permute-start | bytes 1572872 | tf_op jit(solution)/shard_map/ppermute | solution.py:25
  56.7 0.3 select_reduce_fusion
  57.1 0.1 add.76.listed
  57.2 0.2 convert_reduce_fusion.counts
  57.4 0.0 collective-permute-done.refs_0_
  57.4 0.0 collective-permute-done.2.refs_2_
  57.4 2.9 %shard_map.56.before = f32[33,64,256]{2,1,0:T(8,128)S(1)} custom-call(s32[128]{0:T(128)S(1)} %add.76.listed, s32[16]{0:T(128)S(1)} %convert_reduce_fusion.counts, bf16[4,1040,256]{2,1,0:T(8,128)(2,1)S(1)} %all-to-all-done.amps, bf16[4,256,256]{2,1,0:T(8,128)(2,1)S(1)} %collective-permute-done.refs_0_, ...), custom_call_target="tpu_custom_call" | custom-call | flops 268435456 | bytes 8388608 | tf_op jit(solution)/shard_map/pallas_call | solution.py:177
  60.3 6.9 %collective-permute-done.3.held = bf16[4,256,256]{2,1,0:T(8,128)(2,1)} collective-permute-done((bf16[4,256,256]{2,1,0:T(8,128)(2,1)S(1)}, bf16[4,256,256]{2,1,0:T(8,128)(2,1)}, u32[]{:S(2)}, u32[]{:S(2)}) %collective-permute-start.3) | collective-permute-done | bytes 524320 | tf_op jit(solution)/shard_map/ppermute | solution.py:25
  67.2 1.7 %shard_map.57 = bf16[32,64,256]{2,1,0:T(8,128)(2,1)S(1)} custom-call(s32[128]{0:T(128)S(1)} %add.76.listed, s32[16]{0:T(128)S(1)} %convert_reduce_fusion.counts, bf16[4,1040,256]{2,1,0:T(8,128)(2,1)S(1)} %all-to-all-done.amps, f32[33,64,256]{2,1,0:T(8,128)S(1)} %shard_map.56.before, bf16[4,256,256]{2,1,0:T(8,128)(2,1)} %collective-permute-done.3.held), custom_call_target="tpu_custom_call" | custom-call | flops 268435456 | bytes 8388608 | tf_op jit(solution)/shard_map/pallas_call | solution.py:185
  68.8 14.6 %all_to_all.10 = bf16[32,64,256]{2,1,0:T(8,128)(2,1)S(1)} all-to-all(bf16[32,64,256]{2,1,0:T(8,128)(2,1)S(1)} %shard_map.57), channel_id=1, replica_groups={{0,1,2,3},{4,5,6,7},{8,9,10,11},{12,13,14,15},{16,17,18,19},{20,21,22,2..., dimensions={0} | all-to-all | bytes 2097152 | tf_op jit(solution)/shard_map/all_to_all | solution.py:31
  83.4 0.9 %reduce_sum.32 = bf16[8,64,256]{2,1,0:T(8,128)(2,1)} reduce(bf16[4,8,64,256]{3,2,1,0:T(8,128)(2,1)S(1)} %bitcast.10, bf16[]{:T(256)} %constant.105.clone.1), dimensions={0}, to_apply=%region_2.3 | reduce | flops 393216 | bytes 1310722 | tf_op jit(solution)/shard_map/reduce_sum | solution.py:195
  (5 shorter events, 0.0 us)
Async XLA Ops:
  2.5 4.5 %copy-start = (bf16[1,1,256,256]{3,2,1,0:T(8,128)(2,1)S(1)}, bf16[1,1,256,256]{3,2,1,0:T(8,128)(2,1)}, u32[]{:S(2)}) copy-start(bf16[1,1,256,256]{3,2,1,0:T(8,128)(2,1)} %param.6) | copy-start | bytes 393220
  2.5 39.3 %copy-start.1 = (s32[16]{0:T(128)S(1)}, s32[16]{0:T(128)}, u32[]{:S(2)}) copy-start(s32[16]{0:T(128)} %constant.106.clone) | copy-start | bytes 196
  2.5 39.3 %all-to-all-start = ((bf16[4,1040,256]{2,1,0:T(8,128)(2,1)}), bf16[4,1040,256]{2,1,0:T(8,128)(2,1)S(1)}, u32[]{:S(2)}, u32[]{:S(2)}) async-start(bf16[4,1040,256]{2,1,0:T(8,128)(2,1)} %shard_map.55), calls=%async_computation | async-start | bytes 4259840 | tf_op jit(solution)/shard_map/all_to_all | solution.py:31
  41.9 12.9 %collective-permute-start.1 = (bf16[4,256,256]{2,1,0:T(8,128)(2,1)}, bf16[4,256,256]{2,1,0:T(8,128)(2,1)S(1)}, u32[]{:S(2)}, u32[]{:S(2)}) collective-permute-start(bf16[4,256,256]{2,1,0:T(8,128)(2,1)} %bitcast.5), channel_id=1, source_target_pairs={{0,124},{1,125},{2,126},{3,127},{4,64},{5,65},{6,66},{7,67},{8,68}... | collective-permute-start | bytes 1572872 | tf_op jit(solution)/shard_map/ppermute | solution.py:25
  43.8 13.6 %collective-permute-start = (bf16[4,256,256]{2,1,0:T(8,128)(2,1)}, bf16[4,256,256]{2,1,0:T(8,128)(2,1)S(1)}, u32[]{:S(2)}, u32[]{:S(2)}) collective-permute-start(bf16[4,256,256]{2,1,0:T(8,128)(2,1)} %bitcast.5), channel_id=1, source_target_pairs={{0,64},{1,65},{2,66},{3,67},{4,68},{5,69},{6,70},{7,71},{8,72},{9,... | collective-permute-start | bytes 1572872 | tf_op jit(solution)/shard_map/ppermute | solution.py:25
  45.7 11.7 %collective-permute-start.2 = (bf16[4,256,256]{2,1,0:T(8,128)(2,1)}, bf16[4,256,256]{2,1,0:T(8,128)(2,1)}, u32[]{:S(2)}, u32[]{:S(2)}) collective-permute-start(bf16[4,256,256]{2,1,0:T(8,128)(2,1)} %bitcast.5), channel_id=1, source_target_pairs={{0,68},{1,69},{2,70},{3,71},{4,72},{5,73},{6,74},{7,75},{8,76},{9,... | collective-permute-start | bytes 1572872 | tf_op jit(solution)/shard_map/ppermute | solution.py:25
  54.8 12.4 %collective-permute-start.3 = (bf16[4,256,256]{2,1,0:T(8,128)(2,1)S(1)}, bf16[4,256,256]{2,1,0:T(8,128)(2,1)}, u32[]{:S(2)}, u32[]{:S(2)}) collective-permute-start(bf16[4,256,256]{2,1,0:T(8,128)(2,1)S(1)} %collective-permute-done.1.refs_1_), channel_id=1, source_target_pairs={{0,4},{1,5},{2,6},{3,7},{4,8},{5,9},{6,10},{7,11},{8,12},{9,13},{1... | collective-permute-start | bytes 1572872 | tf_op jit(solution)/shard_map/ppermute | solution.py:25

commit v6 on v5

--- a/solution.py
+++ b/solution.py
@@ -147,8 +147,8 @@
     integrals, packed = lax.optimization_barrier((integrals, packed))
     amps = along_x(packed)
     mine = every_fourth(integrals[0])
-    mine, amps = lax.optimization_barrier((mine, amps))
     one, near, other = moved(mine, 1, True), moved(mine, 0, True), moved(mine, -1, True)
+    one, amps = lax.optimization_barrier((one, amps))
     far = moved(one, -1)
 
     numbers = amps[:, flat : flat + 2 * fanout, :own].astype(jnp.int32)

time: 85.6 us -> 85.4 us (level)
  waiting for transfers between devices: 12.7 us -> 14.3 us
  Pallas kernels: 7.09 us -> 5.73 us
    ppermute x4, waiting for transfers between devices: 12.7 us -> 14.3 us  [moved(): return lax.ppermute(block, ('irrep', 'tile'), route)]
    pallas_call x1, Pallas kernels: 2.94 us -> 1.74 us  [per_device(): pl.pallas_call(early, out_shape=jax.ShapeDtypeStruct(total_shape, jnp.flo...]
  transfers between devices with their start and end apart: 5 -> 5, of which waited for: 2 -> 2; matrix products, arithmetic and copies ran while one was open for 1% -> 1% of each run, Pallas kernels for 3% -> 2%
where the time goes in v6:
time: 85.4 us; the launch traced here: 84.7 us
  blocking collectives  49.6 us (58%)
  waiting for transfers between devices  14.3 us (17%)
  starting transfers between devices  12.9 us (15%)
  Pallas kernels  5.73 us (7%)
  other arithmetic  1.56 us (2%)
    all_gather x1, blocking collectives, every_fourth(): lax.all_gather(block, 'tile', axis=0, axis_index_groups=groups, tiled=True)  34.9 us
    all_to_all x1, blocking collectives, along_x(): lax.all_to_all(block, 'tile', split_axis=0, concat_axis=0, axis_index_gro...  14.7 us
    ppermute x4, waiting for transfers between devices, moved(): return lax.ppermute(block, ('irrep', 'tile'), route)  14.3 us
    ppermute x4, starting transfers between devices, moved(): return lax.ppermute(block, ('irrep', 'tile'), route)  8.5 us
    all_to_all x1, starting transfers between devices, along_x(): lax.all_to_all(block, 'tile', split_axis=0, concat_axis=0, axis_index_gro...  4.44 us
    pallas_call x1, Pallas kernels, per_device(): pl.pallas_call(pack, out_shape=jax.ShapeDtypeStruct((XS, flat + META, col...  2.5 us
    pallas_call x1, Pallas kernels, per_device(): pl.pallas_call(early, out_shape=jax.ShapeDtypeStruct(total_shape, jnp.flo...  1.74 us
  transfers between devices with their start and end apart: 5, of which 2 were waited for; matrix products, arithmetic and copies ran while one was open for 1% of the time, Pallas kernels for 2%

profile of v6, /device:TPU:24, one launch (start us, length us, event | category | flops | bytes accessed | tf_op | source)
XLA Modules:
  0.0 84.7 jit_solution(13329565113212066326)
XLA Ops:
  0.0 2.5 %shard_map.55 = bf16[4,1040,256]{2,1,0:T(8,128)(2,1)} custom-call(bf16[1024,256]{1,0:T(8,128)(2,1)} %bitcast.11, s32[2,16]{1,0:T(2,128)} %bitcast.12, s32[2,16]{1,0:T(2,128)} %bitcast.13), custom_call_target="tpu_custom_call" | custom-call | tf_op jit(solution)/shard_map/pallas_call | solution.py:135
  2.5 0.0 copy-start
  2.5 0.0 copy-start.1
  2.5 4.4 %all-to-all-start = ((bf16[4,1040,256]{2,1,0:T(8,128)(2,1)}), bf16[4,1040,256]{2,1,0:T(8,128)(2,1)S(1)}, u32[]{:S(2)}, u32[]{:S(2)}) async-start(bf16[4,1040,256]{2,1,0:T(8,128)(2,1)} %shard_map.55), calls=%async_computation | async-start | bytes 4259840 | tf_op jit(solution)/shard_map/all_to_all | solution.py:31
  7.0 0.0 copy-done
  7.0 34.9 %all-gather = bf16[4,1,256,256]{3,2,1,0:T(8,128)(2,1)} all-gather(bf16[1,1,256,256]{3,2,1,0:T(8,128)(2,1)S(1)} %copy-done), channel_id=2, replica_groups={{0,16,32,48},{1,17,33,49},{2,18,34,50},{3,19,35,51},{4,20,36,52},{5,21,..., dimensions={0}, use_global_device_ids=true | all-gather | bytes 655360 | tf_op jit(solution)/shard_map/all_gather | solution.py:40
  41.8 1.9 %collective-permute-start = (bf16[4,256,256]{2,1,0:T(8,128)(2,1)}, bf16[4,256,256]{2,1,0:T(8,128)(2,1)S(1)}, u32[]{:S(2)}, u32[]{:S(2)}) collective-permute-start(bf16[4,256,256]{2,1,0:T(8,128)(2,1)} %bitcast.5), channel_id=1, source_target_pairs={{0,124},{1,125},{2,126},{3,127},{4,64},{5,65},{6,66},{7,67},{8,68}... | collective-permute-start | bytes 1572872 | tf_op jit(solution)/shard_map/ppermute | solution.py:25
  43.7 1.9 %collective-permute-start.1 = (bf16[4,256,256]{2,1,0:T(8,128)(2,1)}, bf16[4,256,256]{2,1,0:T(8,128)(2,1)S(1)}, u32[]{:S(2)}, u32[]{:S(2)}) collective-permute-start(bf16[4,256,256]{2,1,0:T(8,128)(2,1)} %bitcast.5), channel_id=1, source_target_pairs={{0,64},{1,65},{2,66},{3,67},{4,68},{5,69},{6,70},{7,71},{8,72},{9,... | collective-permute-start | bytes 1572872 | tf_op jit(solution)/shard_map/ppermute | solution.py:25
  45.7 2.8 %collective-permute-start.2 = (bf16[4,256,256]{2,1,0:T(8,128)(2,1)}, bf16[4,256,256]{2,1,0:T(8,128)(2,1)}, u32[]{:S(2)}, u32[]{:S(2)}) collective-permute-start(bf16[4,256,256]{2,1,0:T(8,128)(2,1)} %bitcast.5), channel_id=1, source_target_pairs={{0,68},{1,69},{2,70},{3,71},{4,72},{5,73},{6,74},{7,75},{8,76},{9,... | collective-permute-start | bytes 1572872 | tf_op jit(solution)/shard_map/ppermute | solution.py:25
  48.5 0.0 copy-done.1
  48.5 6.3 %collective-permute-done.refs_1_ = bf16[4,256,256]{2,1,0:T(8,128)(2,1)S(1)} collective-permute-done((bf16[4,256,256]{2,1,0:T(8,128)(2,1)}, bf16[4,256,256]{2,1,0:T(8,128)(2,1)S(1)}, u32[]{:S(2)}, u32[]{:S(2)}) %collective-permute-start) | collective-permute-done | bytes 524320 | tf_op jit(solution)/shard_map/ppermute | solution.py:25
  54.8 0.0 all-to-all-done.amps
  54.8 0.1 eq.40
  54.9 0.1 broadcast_compare_fusion
  54.9 0.2 convolution_convert_fusion
  55.1 0.1 reshape.41
  55.2 1.9 %collective-permute-start.3 = (bf16[4,256,256]{2,1,0:T(8,128)(2,1)S(1)}, bf16[4,256,256]{2,1,0:T(8,128)(2,1)}, u32[]{:S(2)}, u32[]{:S(2)}) collective-permute-start(bf16[4,256,256]{2,1,0:T(8,128)(2,1)S(1)} %collective-permute-done.refs_1_), channel_id=1, source_target_pairs={{0,4},{1,5},{2,6},{3,7},{4,8},{5,9},{6,10},{7,11},{8,12},{9,13},{1... | collective-permute-start | bytes 1572872 | tf_op jit(solution)/shard_map/ppermute | solution.py:25
  57.2 0.3 select_reduce_fusion
  57.5 0.1 add.76.listed
  57.6 0.2 convert_reduce_fusion.counts
  57.8 0.0 collective-permute-done.1.refs_0_
  57.8 0.0 collective-permute-done.2.refs_2_
  57.8 1.7 %shard_map.56.before = f32[33,64,256]{2,1,0:T(8,128)S(1)} custom-call(s32[128]{0:T(128)S(1)} %add.76.listed, s32[16]{0:T(128)S(1)} %convert_reduce_fusion.counts, bf16[4,1040,256]{2,1,0:T(8,128)(2,1)S(1)} %all-to-all-done.amps, bf16[4,256,256]{2,1,0:T(8,128)(2,1)S(1)} %collective-permute-done.1.refs_0_, ...), custom_call_target="tpu_custom_call" | custom-call | flops 268435456 | bytes 8388608 | tf_op jit(solution)/shard_map/pallas_call | solution.py:177
  59.6 8.0 %collective-permute-done.3.held = bf16[4,256,256]{2,1,0:T(8,128)(2,1)} collective-permute-done((bf16[4,256,256]{2,1,0:T(8,128)(2,1)S(1)}, bf16[4,256,256]{2,1,0:T(8,128)(2,1)}, u32[]{:S(2)}, u32[]{:S(2)}) %collective-permute-start.3) | collective-permute-done | bytes 524320 | tf_op jit(solution)/shard_map/ppermute | solution.py:25
  67.6 1.5 %shard_map.57 = bf16[32,64,256]{2,1,0:T(8,128)(2,1)S(1)} custom-call(s32[128]{0:T(128)S(1)} %add.76.listed, s32[16]{0:T(128)S(1)} %convert_reduce_fusion.counts, bf16[4,1040,256]{2,1,0:T(8,128)(2,1)S(1)} %all-to-all-done.amps, f32[33,64,256]{2,1,0:T(8,128)S(1)} %shard_map.56.before, bf16[4,256,256]{2,1,0:T(8,128)(2,1)} %collective-permute-done.3.held), custom_call_target="tpu_custom_call" | custom-call | flops 268435456 | bytes 8388608 | tf_op jit(solution)/shard_map/pallas_call | solution.py:185
  69.1 14.7 %all_to_all.10 = bf16[32,64,256]{2,1,0:T(8,128)(2,1)S(1)} all-to-all(bf16[32,64,256]{2,1,0:T(8,128)(2,1)S(1)} %shard_map.57), channel_id=1, replica_groups={{0,1,2,3},{4,5,6,7},{8,9,10,11},{12,13,14,15},{16,17,18,19},{20,21,22,2..., dimensions={0} | all-to-all | bytes 2097152 | tf_op jit(solution)/shard_map/all_to_all | solution.py:31
  83.8 0.9 %reduce_sum.32 = bf16[8,64,256]{2,1,0:T(8,128)(2,1)} reduce(bf16[4,8,64,256]{3,2,1,0:T(8,128)(2,1)S(1)} %bitcast.10, bf16[]{:T(256)} %constant.105.clone.1), dimensions={0}, to_apply=%region_2.3 | reduce | flops 393216 | bytes 1310722 | tf_op jit(solution)/shard_map/reduce_sum | solution.py:195
  (5 shorter events, 0.0 us)
Async XLA Ops:
  2.5 4.5 %copy-start = (bf16[1,1,256,256]{3,2,1,0:T(8,128)(2,1)S(1)}, bf16[1,1,256,256]{3,2,1,0:T(8,128)(2,1)}, u32[]{:S(2)}) copy-start(bf16[1,1,256,256]{3,2,1,0:T(8,128)(2,1)} %param.6) | copy-start | bytes 393220
  2.5 45.9 %copy-start.1 = (s32[16]{0:T(128)S(1)}, s32[16]{0:T(128)}, u32[]{:S(2)}) copy-start(s32[16]{0:T(128)} %constant.106.clone) | copy-start | bytes 196
  2.5 52.2 %all-to-all-start = ((bf16[4,1040,256]{2,1,0:T(8,128)(2,1)}), bf16[4,1040,256]{2,1,0:T(8,128)(2,1)S(1)}, u32[]{:S(2)}, u32[]{:S(2)}) async-start(bf16[4,1040,256]{2,1,0:T(8,128)(2,1)} %shard_map.55), calls=%async_computation | async-start | bytes 4259840 | tf_op jit(solution)/shard_map/all_to_all | solution.py:31
  41.8 12.9 %collective-permute-start = (bf16[4,256,256]{2,1,0:T(8,128)(2,1)}, bf16[4,256,256]{2,1,0:T(8,128)(2,1)S(1)}, u32[]{:S(2)}, u32[]{:S(2)}) collective-permute-start(bf16[4,256,256]{2,1,0:T(8,128)(2,1)} %bitcast.5), channel_id=1, source_target_pairs={{0,124},{1,125},{2,126},{3,127},{4,64},{5,65},{6,66},{7,67},{8,68}... | collective-permute-start | bytes 1572872 | tf_op jit(solution)/shard_map/ppermute | solution.py:25
  43.7 14.0 %collective-permute-start.1 = (bf16[4,256,256]{2,1,0:T(8,128)(2,1)}, bf16[4,256,256]{2,1,0:T(8,128)(2,1)S(1)}, u32[]{:S(2)}, u32[]{:S(2)}) collective-permute-start(bf16[4,256,256]{2,1,0:T(8,128)(2,1)} %bitcast.5), channel_id=1, source_target_pairs={{0,64},{1,65},{2,66},{3,67},{4,68},{5,69},{6,70},{7,71},{8,72},{9,... | collective-permute-start | bytes 1572872 | tf_op jit(solution)/shard_map/ppermute | solution.py:25
  45.7 12.1 %collective-permute-start.2 = (bf16[4,256,256]{2,1,0:T(8,128)(2,1)}, bf16[4,256,256]{2,1,0:T(8,128)(2,1)}, u32[]{:S(2)}, u32[]{:S(2)}) collective-permute-start(bf16[4,256,256]{2,1,0:T(8,128)(2,1)} %bitcast.5), channel_id=1, source_target_pairs={{0,68},{1,69},{2,70},{3,71},{4,72},{5,73},{6,74},{7,75},{8,76},{9,... | collective-permute-start | bytes 1572872 | tf_op jit(solution)/shard_map/ppermute | solution.py:25
  55.2 12.4 %collective-permute-start.3 = (bf16[4,256,256]{2,1,0:T(8,128)(2,1)S(1)}, bf16[4,256,256]{2,1,0:T(8,128)(2,1)}, u32[]{:S(2)}, u32[]{:S(2)}) collective-permute-start(bf16[4,256,256]{2,1,0:T(8,128)(2,1)S(1)} %collective-permute-done.refs_1_), channel_id=1, source_target_pairs={{0,4},{1,5},{2,6},{3,7},{4,8},{5,9},{6,10},{7,11},{8,12},{9,13},{1... | collective-permute-start | bytes 1572872 | tf_op jit(solution)/shard_map/ppermute | solution.py:25

commit v7 on v6

--- a/solution.py
+++ b/solution.py
@@ -76,7 +76,7 @@
         copy.wait()
 
 
-def add_products(first, listed, counts, amps, held, total):
+def add_products(first, listed, counts, amps, held, total, before=None):
     rows = total.shape[1]
     own = (amps.shape[1] - META) // rows
     tiles = [(ref, k) for ref in held for k in range(ref.shape[0])]
@@ -97,7 +97,10 @@
             total[code & 63] += product[i * rows : (i + 1) * rows]
 
     for low in range(first, first + len(tiles), 4):
-        for codes, product in [pair(place, 0) for place in range(low, low + 4)]:
+        products = [pair(place, 0) for place in range(low, low + 4)]
+        if before is not None and low == first:
+            total[...] = before[...]
+        for codes, product in products:
             add(codes, product)
     for place in range(first, first + len(tiles)):
 
@@ -115,8 +118,7 @@
 
 
 def late(first, listed, counts, amps, before, held, out, total):
-    total[...] = before[...]
-    add_products(first, listed, counts, amps, (held,), total)
+    add_products(first, listed, counts, amps, (held,), total, before)
     out[...] = total[: out.shape[0]].astype(out.dtype)
 
 

time: 85.4 us -> 85.5 us (level)
  no operation moved by 1% of the time
where the time goes in v7:
time: 85.5 us; the launch traced here: 84 us
  blocking collectives  48.8 us (57%)
  waiting for transfers between devices  14 us (16%)
  starting transfers between devices  12.9 us (15%)
  Pallas kernels  6.05 us (7%)
  other arithmetic  1.56 us (2%)
    all_gather x1, blocking collectives, every_fourth(): lax.all_gather(block, 'tile', axis=0, axis_index_groups=groups, tiled=True)  34.9 us
    ppermute x4, waiting for transfers between devices, moved(): return lax.ppermute(block, ('irrep', 'tile'), route)  14 us
    all_to_all x1, blocking collectives, along_x(): lax.all_to_all(block, 'tile', split_axis=0, concat_axis=0, axis_index_gro...  14 us
    ppermute x4, starting transfers between devices, moved(): return lax.ppermute(block, ('irrep', 'tile'), route)  8.5 us
    all_to_all x1, starting transfers between devices, along_x(): lax.all_to_all(block, 'tile', split_axis=0, concat_axis=0, axis_index_gro...  4.44 us
    pallas_call x1, Pallas kernels, per_device(): pl.pallas_call(pack, out_shape=jax.ShapeDtypeStruct((XS, flat + META, col...  2.5 us
    pallas_call x1, Pallas kernels, per_device(): pl.pallas_call(early, out_shape=jax.ShapeDtypeStruct(total_shape, jnp.flo...  2.07 us
  transfers between devices with their start and end apart: 5, of which 2 were waited for; matrix products, arithmetic and copies ran while one was open for 1% of the time, Pallas kernels for 2%

profile of v7, /device:TPU:24, one launch (start us, length us, event | category | flops | bytes accessed | tf_op | source)
XLA Modules:
  0.0 84.0 jit_solution(13246418191544561998)
XLA Ops:
  0.0 2.5 %shard_map.55 = bf16[4,1040,256]{2,1,0:T(8,128)(2,1)} custom-call(bf16[1024,256]{1,0:T(8,128)(2,1)} %bitcast.11, s32[2,16]{1,0:T(2,128)} %bitcast.12, s32[2,16]{1,0:T(2,128)} %bitcast.13), custom_call_target="tpu_custom_call" | custom-call | tf_op jit(solution)/shard_map/pallas_call | solution.py:137
  2.5 0.0 copy-start
  2.5 0.0 copy-start.1
  2.5 4.4 %all-to-all-start = ((bf16[4,1040,256]{2,1,0:T(8,128)(2,1)}), bf16[4,1040,256]{2,1,0:T(8,128)(2,1)S(1)}, u32[]{:S(2)}, u32[]{:S(2)}) async-start(bf16[4,1040,256]{2,1,0:T(8,128)(2,1)} %shard_map.55), calls=%async_computation | async-start | bytes 4259840 | tf_op jit(solution)/shard_map/all_to_all | solution.py:31
  7.0 0.0 copy-done
  7.0 34.9 %all-gather = bf16[4,1,256,256]{3,2,1,0:T(8,128)(2,1)} all-gather(bf16[1,1,256,256]{3,2,1,0:T(8,128)(2,1)S(1)} %copy-done), channel_id=2, replica_groups={{0,16,32,48},{1,17,33,49},{2,18,34,50},{3,19,35,51},{4,20,36,52},{5,21,..., dimensions={0}, use_global_device_ids=true | all-gather | bytes 655360 | tf_op jit(solution)/shard_map/all_gather | solution.py:40
  41.8 1.9 %collective-permute-start = (bf16[4,256,256]{2,1,0:T(8,128)(2,1)}, bf16[4,256,256]{2,1,0:T(8,128)(2,1)S(1)}, u32[]{:S(2)}, u32[]{:S(2)}) collective-permute-start(bf16[4,256,256]{2,1,0:T(8,128)(2,1)} %bitcast.5), channel_id=1, source_target_pairs={{0,124},{1,125},{2,126},{3,127},{4,64},{5,65},{6,66},{7,67},{8,68}... | collective-permute-start | bytes 1572872 | tf_op jit(solution)/shard_map/ppermute | solution.py:25
  43.7 1.9 %collective-permute-start.1 = (bf16[4,256,256]{2,1,0:T(8,128)(2,1)}, bf16[4,256,256]{2,1,0:T(8,128)(2,1)S(1)}, u32[]{:S(2)}, u32[]{:S(2)}) collective-permute-start(bf16[4,256,256]{2,1,0:T(8,128)(2,1)} %bitcast.5), channel_id=1, source_target_pairs={{0,64},{1,65},{2,66},{3,67},{4,68},{5,69},{6,70},{7,71},{8,72},{9,... | collective-permute-start | bytes 1572872 | tf_op jit(solution)/shard_map/ppermute | solution.py:25
  45.7 2.8 %collective-permute-start.2 = (bf16[4,256,256]{2,1,0:T(8,128)(2,1)}, bf16[4,256,256]{2,1,0:T(8,128)(2,1)}, u32[]{:S(2)}, u32[]{:S(2)}) collective-permute-start(bf16[4,256,256]{2,1,0:T(8,128)(2,1)} %bitcast.5), channel_id=1, source_target_pairs={{0,68},{1,69},{2,70},{3,71},{4,72},{5,73},{6,74},{7,75},{8,76},{9,... | collective-permute-start | bytes 1572872 | tf_op jit(solution)/shard_map/ppermute | solution.py:25
  48.5 0.0 copy-done.1
  48.5 6.3 %collective-permute-done.refs_1_ = bf16[4,256,256]{2,1,0:T(8,128)(2,1)S(1)} collective-permute-done((bf16[4,256,256]{2,1,0:T(8,128)(2,1)}, bf16[4,256,256]{2,1,0:T(8,128)(2,1)S(1)}, u32[]{:S(2)}, u32[]{:S(2)}) %collective-permute-start) | collective-permute-done | bytes 524320 | tf_op jit(solution)/shard_map/ppermute | solution.py:25
  54.8 0.0 all-to-all-done.amps
  54.8 0.1 eq.40
  54.9 0.1 broadcast_compare_fusion
  54.9 0.2 convolution_convert_fusion
  55.1 0.1 reshape.41
  55.2 1.9 %collective-permute-start.3 = (bf16[4,256,256]{2,1,0:T(8,128)(2,1)S(1)}, bf16[4,256,256]{2,1,0:T(8,128)(2,1)}, u32[]{:S(2)}, u32[]{:S(2)}) collective-permute-start(bf16[4,256,256]{2,1,0:T(8,128)(2,1)S(1)} %collective-permute-done.refs_1_), channel_id=1, source_target_pairs={{0,4},{1,5},{2,6},{3,7},{4,8},{5,9},{6,10},{7,11},{8,12},{9,13},{1... | collective-permute-start | bytes 1572872 | tf_op jit(solution)/shard_map/ppermute | solution.py:25
  57.2 0.3 select_reduce_fusion
  57.5 0.1 add.76.listed
  57.6 0.2 convert_reduce_fusion.counts
  57.8 0.0 collective-permute-done.1.refs_0_
  57.8 0.0 collective-permute-done.2.refs_2_
  57.8 2.1 %shard_map.56.before = f32[33,64,256]{2,1,0:T(8,128)S(1)} custom-call(s32[128]{0:T(128)S(1)} %add.76.listed, s32[16]{0:T(128)S(1)} %convert_reduce_fusion.counts, bf16[4,1040,256]{2,1,0:T(8,128)(2,1)S(1)} %all-to-all-done.amps, bf16[4,256,256]{2,1,0:T(8,128)(2,1)S(1)} %collective-permute-done.1.refs_0_, ...), custom_call_target="tpu_custom_call" | custom-call | flops 268435456 | bytes 8388608 | tf_op jit(solution)/shard_map/pallas_call | solution.py:179
  59.9 7.7 %collective-permute-done.3.held = bf16[4,256,256]{2,1,0:T(8,128)(2,1)} collective-permute-done((bf16[4,256,256]{2,1,0:T(8,128)(2,1)S(1)}, bf16[4,256,256]{2,1,0:T(8,128)(2,1)}, u32[]{:S(2)}, u32[]{:S(2)}) %collective-permute-start.3) | collective-permute-done | bytes 524320 | tf_op jit(solution)/shard_map/ppermute | solution.py:25
  67.6 1.5 %shard_map.57 = bf16[32,64,256]{2,1,0:T(8,128)(2,1)S(1)} custom-call(s32[128]{0:T(128)S(1)} %add.76.listed, s32[16]{0:T(128)S(1)} %convert_reduce_fusion.counts, bf16[4,1040,256]{2,1,0:T(8,128)(2,1)S(1)} %all-to-all-done.amps, f32[33,64,256]{2,1,0:T(8,128)S(1)} %shard_map.56.before, bf16[4,256,256]{2,1,0:T(8,128)(2,1)} %collective-permute-done.3.held), custom_call_target="tpu_custom_call" | custom-call | flops 268435456 | bytes 8388608 | tf_op jit(solution)/shard_map/pallas_call | solution.py:187
  69.1 14.0 %all_to_all.10 = bf16[32,64,256]{2,1,0:T(8,128)(2,1)S(1)} all-to-all(bf16[32,64,256]{2,1,0:T(8,128)(2,1)S(1)} %shard_map.57), channel_id=1, replica_groups={{0,1,2,3},{4,5,6,7},{8,9,10,11},{12,13,14,15},{16,17,18,19},{20,21,22,2..., dimensions={0} | all-to-all | bytes 2097152 | tf_op jit(solution)/shard_map/all_to_all | solution.py:31
  83.1 0.9 %reduce_sum.32 = bf16[8,64,256]{2,1,0:T(8,128)(2,1)} reduce(bf16[4,8,64,256]{3,2,1,0:T(8,128)(2,1)S(1)} %bitcast.10, bf16[]{:T(256)} %constant.105.clone.1), dimensions={0}, to_apply=%region_2.3 | reduce | flops 393216 | bytes 1310722 | tf_op jit(solution)/shard_map/reduce_sum | solution.py:197
  (5 shorter events, 0.0 us)
Async XLA Ops:
  2.5 4.5 %copy-start = (bf16[1,1,256,256]{3,2,1,0:T(8,128)(2,1)S(1)}, bf16[1,1,256,256]{3,2,1,0:T(8,128)(2,1)}, u32[]{:S(2)}) copy-start(bf16[1,1,256,256]{3,2,1,0:T(8,128)(2,1)} %param.6) | copy-start | bytes 393220
  2.5 45.9 %copy-start.1 = (s32[16]{0:T(128)S(1)}, s32[16]{0:T(128)}, u32[]{:S(2)}) copy-start(s32[16]{0:T(128)} %constant.106.clone) | copy-start | bytes 196
  2.5 52.2 %all-to-all-start = ((bf16[4,1040,256]{2,1,0:T(8,128)(2,1)}), bf16[4,1040,256]{2,1,0:T(8,128)(2,1)S(1)}, u32[]{:S(2)}, u32[]{:S(2)}) async-start(bf16[4,1040,256]{2,1,0:T(8,128)(2,1)} %shard_map.55), calls=%async_computation | async-start | bytes 4259840 | tf_op jit(solution)/shard_map/all_to_all | solution.py:31
  41.8 12.9 %collective-permute-start = (bf16[4,256,256]{2,1,0:T(8,128)(2,1)}, bf16[4,256,256]{2,1,0:T(8,128)(2,1)S(1)}, u32[]{:S(2)}, u32[]{:S(2)}) collective-permute-start(bf16[4,256,256]{2,1,0:T(8,128)(2,1)} %bitcast.5), channel_id=1, source_target_pairs={{0,124},{1,125},{2,126},{3,127},{4,64},{5,65},{6,66},{7,67},{8,68}... | collective-permute-start | bytes 1572872 | tf_op jit(solution)/shard_map/ppermute | solution.py:25
  43.7 14.0 %collective-permute-start.1 = (bf16[4,256,256]{2,1,0:T(8,128)(2,1)}, bf16[4,256,256]{2,1,0:T(8,128)(2,1)S(1)}, u32[]{:S(2)}, u32[]{:S(2)}) collective-permute-start(bf16[4,256,256]{2,1,0:T(8,128)(2,1)} %bitcast.5), channel_id=1, source_target_pairs={{0,64},{1,65},{2,66},{3,67},{4,68},{5,69},{6,70},{7,71},{8,72},{9,... | collective-permute-start | bytes 1572872 | tf_op jit(solution)/shard_map/ppermute | solution.py:25
  45.7 12.1 %collective-permute-start.2 = (bf16[4,256,256]{2,1,0:T(8,128)(2,1)}, bf16[4,256,256]{2,1,0:T(8,128)(2,1)}, u32[]{:S(2)}, u32[]{:S(2)}) collective-permute-start(bf16[4,256,256]{2,1,0:T(8,128)(2,1)} %bitcast.5), channel_id=1, source_target_pairs={{0,68},{1,69},{2,70},{3,71},{4,72},{5,73},{6,74},{7,75},{8,76},{9,... | collective-permute-start | bytes 1572872 | tf_op jit(solution)/shard_map/ppermute | solution.py:25
  55.2 12.4 %collective-permute-start.3 = (bf16[4,256,256]{2,1,0:T(8,128)(2,1)S(1)}, bf16[4,256,256]{2,1,0:T(8,128)(2,1)}, u32[]{:S(2)}, u32[]{:S(2)}) collective-permute-start(bf16[4,256,256]{2,1,0:T(8,128)(2,1)S(1)} %collective-permute-done.refs_1_), channel_id=1, source_target_pairs={{0,4},{1,5},{2,6},{3,7},{4,8},{5,9},{6,10},{7,11},{8,12},{9,13},{1... | collective-permute-start | bytes 1572872 | tf_op jit(solution)/shard_map/ppermute | solution.py:25
